TPU v7x, 32 devices: a whole 2x2x4 slice. The times are simulated.
32 devices in a mesh: groups: 2 (over y), air: 4 (over z), plate: 2 (over x), field: 2 (over core).
Axes of the slice: x: 2, y: 2, z: 4, core: 2. Of those that a mesh axis runs over, the one named last changes fastest.
Arguments:
- air_prev: float32 [128, 256, 256], P(('groups', 'air'), 'plate', 'field'), parts along dimension 0, may hold values from -3 to 3
- air_now: float32 [128, 256, 256], P(('groups', 'air'), 'plate', 'field'), parts along dimension 0, may hold values from -3 to 3
- plate_prev: float32 [6, 64, 256], P('groups', 'air', 'plate'), parts along dimension 0, may hold values from -3 to 3
- plate_now: float32 [6, 64, 256], P('groups', 'air', 'plate'), parts along dimension 0, may hold values from -3 to 3
- plate_height: int32 [6], P('groups'), parts along dimension 0, may hold values from 2 to 253
- plate_rows: int32 [6, 2], P('groups'), parts along dimension 0, may hold values from 0 to 64, as said below
- plate_cols: int32 [6, 2], P('groups'), parts along dimension 0, may hold values from 0 to 256, as said below
Outputs:
- pressure_after: float32 [128, 256, 256], P(('groups', 'air'), 'plate', 'field'), parts along dimension 0
- pressure_before: float32 [128, 256, 256], P(('groups', 'air'), 'plate', 'field'), parts along dimension 0
- plate_after: float32 [6, 64, 256], P('groups', 'air', 'plate'), parts along dimension 0
- plate_before: float32 [6, 64, 256], P('groups', 'air', 'plate'), parts along dimension 0
There are 2 independent parts, one for each index of `groups`. A program takes and returns all parts, laid end to end along the dimension named above; each array names one. Nothing has to cross between parts.
Inputs may be any that keep to these rules, and one draw needn't show every extreme that they name: `plate_rows`: row k holds a plate's first covered index and one past its last; the first lies below 16, the other at or above 48. `plate_cols`: row k holds a plate's first covered index and one past its last; the first lies below 64, the other at or above 192.
All inputs are finite; a program needn't handle non-finite values.
Results may differ from a plain program's by a relative error of at most 0.00002.
Values sent between devices are 32-bit elements; how exact they have to be, the bound alone decides.
A program may use at most 64 MiB of HBM per device.

v0:
```python
import jax
import jax.numpy as jnp
from jax import lax
from jax.sharding import PartitionSpec as P

near_weight = 16.0 / 12.0
far_weight = 1.0 / 12.0
centre_weight = 7.5
air_step = 0.2
plate_step = 0.05
plate_load = 0.3
air_drive = 0.1


def padded_2(block, sides, width):
    for axis, dim in sides:
        count = lax.axis_size(axis)
        forward = [(i, i + 1) for i in range(count - 1)]
        backward = [(target, source) for source, target in forward]
        low = lax.ppermute(
            lax.slice_in_dim(block, block.shape[dim] - width, None, axis=dim), axis, forward
        )
        high = lax.ppermute(lax.slice_in_dim(block, 0, width, axis=dim), axis, backward)
        block = jnp.concatenate([low, block, high], axis=dim)
    return block


def lap_inner(padded):
    size_row = padded.shape[0] - 4
    size_col = padded.shape[1] - 4
    size_depth = padded.shape[2] - 4

    def window(offset_row, offset_col, offset_depth):
        return padded[
            offset_row : offset_row + size_row,
            offset_col : offset_col + size_col,
            offset_depth : offset_depth + size_depth,
        ]

    nearest = (
        window(1, 2, 2)
        + window(3, 2, 2)
        + (window(2, 1, 2) + window(2, 3, 2))
        + (window(2, 2, 1) + window(2, 2, 3))
    )
    farther = (
        window(0, 2, 2)
        + window(4, 2, 2)
        + (window(2, 0, 2) + window(2, 4, 2))
        + (window(2, 2, 0) + window(2, 2, 4))
    )
    return near_weight * nearest - far_weight * farther - centre_weight * window(2, 2, 2)


def bih_inner(padded):
    size_row = padded.shape[1] - 4
    size_col = padded.shape[2] - 4

    def window(offset_row, offset_col):
        return padded[:, offset_row : offset_row + size_row, offset_col : offset_col + size_col]

    axial_terms = window(1, 2) + window(3, 2) + (window(2, 1) + window(2, 3))
    diagonal = window(1, 1) + window(1, 3) + (window(3, 1) + window(3, 3))
    distant = window(0, 2) + window(4, 2) + (window(2, 0) + window(2, 4))
    return 20.0 * window(2, 2) - 8.0 * axial_terms + 2.0 * diagonal + distant


def plate_mask(plate_rows, plate_cols, row_start, col_start, row_count, col_count):
    row_index = row_start + jnp.arange(row_count, dtype=jnp.int32)
    col_index = col_start + jnp.arange(col_count, dtype=jnp.int32)
    inside_rows = (row_index[None, :] >= plate_rows[:, 0:1]) & (
        row_index[None, :] < plate_rows[:, 1:2]
    )
    inside_cols = (col_index[None, :] >= plate_cols[:, 0:1]) & (
        col_index[None, :] < plate_cols[:, 1:2]
    )
    return (inside_rows[:, :, None] & inside_cols[:, None, :]).astype(jnp.float32)


def layer_jump(padded, depth_anchor, plate_height, own_low, own_high):
    interior = padded[2:-2, 2:-2, :]
    deepest = interior.shape[2] - 1
    values = []
    for number in range(plate_height.shape[0]):
        height = plate_height[number]
        upper_index = jnp.clip(height + 1 - depth_anchor, 0, deepest)
        lower_index = jnp.clip(height - 1 - depth_anchor, 0, deepest)
        upper_values = lax.dynamic_index_in_dim(interior, upper_index, 2, keepdims=False)
        lower_values = lax.dynamic_index_in_dim(interior, lower_index, 2, keepdims=False)
        owns_plate = (height >= own_low) & (height < own_high)
        values.append(jnp.where(owns_plate, upper_values - lower_values, 0.0))
    return jnp.stack(values)


def advance(air_back, air_padded, plate_back, plate_padded, tables, anchor, own_bounds):
    plate_rows, plate_cols, plate_height = tables
    row_start, col_start, depth_start = anchor
    local_jump = layer_jump(air_padded, depth_start - 2, plate_height, own_bounds[0], own_bounds[1])
    jump = lax.psum(local_jump, "field")
    plate_centre = plate_padded[:, 2:-2, 2:-2]
    mask = plate_mask(
        plate_rows, plate_cols, row_start, col_start, plate_centre.shape[1], plate_centre.shape[2]
    )
    plate_next = mask * (
        2.0 * plate_centre - plate_back - plate_step * bih_inner(plate_padded) - plate_load * jump
    )
    motion = plate_next - plate_centre
    air_centre = air_padded[2:-2, 2:-2, 2:-2]
    depth_index = depth_start + jnp.arange(air_centre.shape[2], dtype=jnp.int32)
    air_next = 2.0 * air_centre - air_back + air_step * lap_inner(air_padded)
    source = jnp.zeros(air_centre.shape, jnp.float32)
    for number in range(plate_height.shape[0]):
        profile = (depth_index == plate_height[number] + 1).astype(jnp.float32) - (
            depth_index == plate_height[number] - 1
        ).astype(jnp.float32)
        source = source + motion[number][:, :, None] * profile[None, None, :]
    air_next = air_next + air_drive * source
    return (air_next, plate_next)


def on_device(air_prev, air_now, plate_prev, plate_now, plate_height, plate_rows, plate_cols):
    slab_rows, slab_cols, slab_depth = air_now.shape
    row_start = lax.axis_index("air") * slab_rows
    col_start = lax.axis_index("plate") * slab_cols
    depth_start = lax.axis_index("field") * slab_depth
    tables = (plate_rows, plate_cols, plate_height)
    own_bounds = (depth_start, depth_start + slab_depth)
    own_mask = plate_mask(plate_rows, plate_cols, row_start, col_start, slab_rows, slab_cols)
    plate_first = own_mask * plate_prev
    plate_second = own_mask * plate_now
    anchor = (row_start, col_start, depth_start)

    def one_step(air_back, air_centre, plate_back, plate_centre):
        air_padded = padded_2(air_centre, (("air", 0), ("plate", 1), ("field", 2)), 2)
        plate_padded = padded_2(plate_centre, (("air", 1), ("plate", 2)), 2)
        return advance(air_back, air_padded, plate_back, plate_padded, tables, anchor, own_bounds)

    air_third, plate_third = one_step(air_prev, air_now, plate_first, plate_second)
    air_fourth, plate_fourth = one_step(air_now, air_third, plate_second, plate_third)
    return (air_fourth, air_third, plate_fourth, plate_third)


def solution(mesh):
    placed = (
        P(("groups", "air"), "plate", "field"),
        P(("groups", "air"), "plate", "field"),
        P("groups", "air", "plate"),
        P("groups", "air", "plate"),
        P("groups"),
        P("groups", None),
        P("groups", None),
    )
    return jax.shard_map(
        on_device,
        mesh=mesh,
        in_specs=placed,
        out_specs=(
            P(("groups", "air"), "plate", "field"),
            P(("groups", "air"), "plate", "field"),
            P("groups", "air", "plate"),
            P("groups", "air", "plate"),
        ),
        check_vma=False,
    )
```

profile of v0, /device:TPU:0, one launch (start us, length us, event | category | flops | bytes accessed | tf_op | source)
XLA Modules:
  0.0 123.6 jit_solution(13881206483604646490)
XLA Ops:
  0.6 0.0 copy-start.2
  0.6 1.1 fusion.72
  1.7 4.9 %collective-permute-start = (f32[2,128,128]{2,1,0:T(8,128)S(1)}, f32[2,128,128]{2,1,0:T(8,128)S(1)}, u32[]{:S(2)}, u32[]{:S(2)}) collective-permute-start(f32[2,128,128]{2,1,0:T(8,128)S(1)} %get-tuple-element.34), channel_id=1, source_target_pairs={{0,4},{4,8},{8,12},{1,5},{5,9},{9,13},{2,6},{6,10},{10,14},{3,7},{... | collective-permute-start | bytes 393224 | tf_op jit(solution)/shard_map/ppermute | solution.py:20
  6.7 1.3 %collective-permute-start.1 = (f32[2,128,128]{2,1,0:T(8,128)S(1)}, f32[2,128,128]{2,1,0:T(8,128)S(1)}, u32[]{:S(2)}, u32[]{:S(2)}) collective-permute-start(f32[2,128,128]{2,1,0:T(8,128)S(1)} %get-tuple-element.33), channel_id=1, source_target_pairs={{4,0},{8,4},{12,8},{5,1},{9,5},{13,9},{6,2},{10,6},{14,10},{7,3},{... | collective-permute-start | bytes 393224 | tf_op jit(solution)/shard_map/ppermute | solution.py:23
  8.0 0.8 slice_bitcast_fusion.7
  8.7 0.8 slice_bitcast_fusion.9
  9.5 0.1 compare_and_fusion
  9.6 0.1 compare_and_fusion.1
  9.7 0.8 and_select_fusion.3
  10.5 4.5 %collective-permute-start.6 = (f32[3,2,128]{2,1,0:T(2,128)S(1)}, f32[3,2,128]{2,1,0:T(2,128)S(1)}, u32[]{:S(2)}, u32[]{:S(2)}) collective-permute-start(f32[3,2,128]{2,1,0:T(2,128)S(1)} %get-tuple-element.55), channel_id=1, source_target_pairs={{0,4},{4,8},{8,12},{1,5},{5,9},{9,13},{2,6},{6,10},{10,14},{3,7},{... | collective-permute-start | bytes 9224 | tf_op jit(solution)/shard_map/ppermute | solution.py:20
  15.0 1.3 %collective-permute-start.7 = (f32[3,2,128]{2,1,0:T(2,128)S(1)}, f32[3,2,128]{2,1,0:T(2,128)S(1)}, u32[]{:S(2)}, u32[]{:S(2)}) collective-permute-start(f32[3,2,128]{2,1,0:T(2,128)S(1)} %get-tuple-element.56), channel_id=1, source_target_pairs={{4,0},{8,4},{12,8},{5,1},{9,5},{13,9},{6,2},{10,6},{14,10},{7,3},{... | collective-permute-start | bytes 9224 | tf_op jit(solution)/shard_map/ppermute | solution.py:23
  16.3 1.4 %fusion.77 = (s32[1]{0:T(128)}, s32[1]{0:T(128)}, s32[1]{0:T(128)}) fusion(s32[3]{0:T(128)} %param.11), kind=kLoop, calls=%fused_computation.188 | loop fusion | bytes 24 | tf_op jit(solution)/shard_map/slice | solution.py:85
  21.6 0.6 fusion.65
  26.1 0.0 collective-permute-done.6
  26.2 0.4 constant_dynamic-update-slice_fusion
  26.7 3.4 %collective-permute-start.2 = (f32[20,2,128]{2,1,0:T(2,128)S(1)}, f32[20,2,128]{2,1,0:T(2,128)S(1)}, u32[]{:S(2)}, u32[]{:S(2)}) collective-permute-start(f32[20,2,128]{2,1,0:T(2,128)S(1)} %get-tuple-element.20), channel_id=1, source_target_pairs={{0,2},{1,3},{4,6},{5,7},{8,10},{9,11},{12,14},{13,15},{16,18},{17,... | collective-permute-start | bytes 61448 | tf_op jit(solution)/shard_map/ppermute | solution.py:20
  30.1 1.3 %collective-permute-start.3 = (f32[20,2,128]{2,1,0:T(2,128)S(1)}, f32[20,2,128]{2,1,0:T(2,128)S(1)}, u32[]{:S(2)}, u32[]{:S(2)}) collective-permute-start(f32[20,2,128]{2,1,0:T(2,128)S(1)} %get-tuple-element.21), channel_id=1, source_target_pairs={{2,0},{3,1},{6,4},{7,5},{10,8},{11,9},{14,12},{15,13},{18,16},{19,... | collective-permute-start | bytes 61448 | tf_op jit(solution)/shard_map/ppermute | solution.py:23
  31.4 0.1 fusion.74
  31.5 4.5 %collective-permute-start.8 = (f32[3,20,2]{2,1,0:T(8,128)S(1)}, f32[3,20,2]{2,1,0:T(8,128)S(1)}, u32[]{:S(2)}, u32[]{:S(2)}) collective-permute-start(f32[3,20,2]{2,1,0:T(8,128)S(1)} %get-tuple-element.41), channel_id=1, source_target_pairs={{0,2},{1,3},{4,6},{5,7},{8,10},{9,11},{12,14},{13,15},{16,18},{17,... | collective-permute-start | bytes 1448 | tf_op jit(solution)/shard_map/ppermute | solution.py:20
  36.0 1.3 %collective-permute-start.9 = (f32[3,20,2]{2,1,0:T(8,128)S(1)}, f32[3,20,2]{2,1,0:T(8,128)}, u32[]{:S(2)}, u32[]{:S(2)}) collective-permute-start(f32[3,20,2]{2,1,0:T(8,128)S(1)} %get-tuple-element.42), channel_id=1, source_target_pairs={{2,0},{3,1},{6,4},{7,5},{10,8},{11,9},{14,12},{15,13},{18,16},{19,... | collective-permute-start | bytes 1448 | tf_op jit(solution)/shard_map/ppermute | solution.py:23
  37.4 1.2 pad_maximum_fusion
  38.6 2.5 %copy.31 = f32[20,132,128]{1,0,2:T(8,128)S(1)} copy(f32[20,132,128]{2,1,0:T(8,128)} %pad_maximum_fusion) | data formatting | bytes 2703360 | tf_op jit(solution)/shard_map/concatenate | solution.py:24
  41.1 1.3 %collective-permute-start.4 = (f32[20,132,2]{1,0,2:T(8,128)S(1)}, f32[20,132,2]{1,0,2:T(8,128)S(1)}, u32[]{:S(2)}, u32[]{:S(2)}) collective-permute-start(f32[20,132,2]{1,0,2:T(8,128)S(1)} %get-tuple-element.14), channel_id=1, source_target_pairs={{0,1},{2,3},{4,5},{6,7},{8,9},{10,11},{12,13},{14,15},{16,17},{18,... | collective-permute-start | bytes 63368 | tf_op jit(solution)/shard_map/ppermute | solution.py:20
  42.4 1.3 %collective-permute-start.5 = (f32[20,132,2]{1,0,2:T(8,128)S(1)}, f32[20,132,2]{1,0,2:T(8,128)S(1)}, u32[]{:S(2)}, u32[]{:S(2)}) collective-permute-start(f32[20,132,2]{1,0,2:T(8,128)S(1)} %get-tuple-element.15), channel_id=1, source_target_pairs={{1,0},{3,2},{5,4},{7,6},{9,8},{11,10},{13,12},{15,14},{17,16},{19,... | collective-permute-start | bytes 63368 | tf_op jit(solution)/shard_map/ppermute | solution.py:23
  43.7 0.0 copy-start.17
  43.7 0.6 copy-done.17
  44.3 0.9 maximum_maximum_fusion.1
  45.2 0.3 collective-permute-done.5
  45.5 0.4 pad_maximum_fusion.5
  45.9 4.1 %psum.14 = f32[3,16,128]{2,1,0:T(8,128)S(1)} all-reduce(f32[3,16,128]{2,1,0:T(8,128)S(1)} %pad_maximum_fusion.35), channel_id=1, replica_groups=mesh['groups'=2,'air'=4,'plate'=2,'field'=2] {'field'}, use_global_device_ids=true, to_apply=%region_0.1 | all-reduce | flops 6144 | bytes 49152 | tf_op jit(solution)/shard_map/psum | solution.py:99
  50.0 0.9 fusion.67
  50.9 0.0 copy-start.10
  50.9 4.5 %collective-permute-start.16 = (f32[3,2,128]{2,1,0:T(2,128)S(1)}, f32[3,2,128]{2,1,0:T(2,128)S(1)}, u32[]{:S(2)}, u32[]{:S(2)}) collective-permute-start(f32[3,2,128]{2,1,0:T(2,128)S(1)} %get-tuple-element.50), channel_id=1, source_target_pairs={{0,4},{4,8},{8,12},{1,5},{5,9},{9,13},{2,6},{6,10},{10,14},{3,7},{... | collective-permute-start | bytes 9224 | tf_op jit(solution)/shard_map/ppermute | solution.py:20
  55.5 1.3 %collective-permute-start.17 = (f32[3,2,128]{2,1,0:T(2,128)S(1)}, f32[3,2,128]{2,1,0:T(2,128)S(1)}, u32[]{:S(2)}, u32[]{:S(2)}) collective-permute-start(f32[3,2,128]{2,1,0:T(2,128)S(1)} %get-tuple-element.51), channel_id=1, source_target_pairs={{4,0},{8,4},{12,8},{5,1},{9,5},{13,9},{6,2},{10,6},{14,10},{7,3},{... | collective-permute-start | bytes 9224 | tf_op jit(solution)/shard_map/ppermute | solution.py:23
  56.8 0.0 copy-start.3
  56.8 1.6 %copy.32 = f32[20,132,2]{2,1,0:T(8,128)} copy(f32[20,132,2]{1,0,2:T(8,128)S(1)} %collective-permute-done.4) | data formatting | bytes 42240 | tf_op jit(solution)/shard_map/ppermute | solution.py:20
  58.5 1.6 %copy.34 = f32[20,132,2]{2,1,0:T(8,128)} copy(f32[20,132,2]{1,0,2:T(8,128)S(1)} %collective-permute-done.5) | data formatting | bytes 42240 | tf_op jit(solution)/shard_map/ppermute | solution.py:23
  60.1 10.1 %fusion.20 = f32[16,128,128]{2,1,0:T(8,128)S(1)} fusion(f32[20,128,128]{2,1,0:T(8,128)} %copy-done.6, f32[20,2,128]{2,1,0:T(2,128)S(1)} %collective-permute-done.3, f32[20,2,128]{2,1,0:T(2,128)S(1)} %collective-permute-done.2, f32[20,132,2]{2,1,0:T(8,128)} %copy.34, f32[20,132,2]{2,1,0:T(8,128)} %copy.32, f32[18,128,128]{2,1,0:T(8,128)S(1)} %copy-done.5, ...), kind=kLoop, calls=%fused_computation.36 | loop fusion | flops 11010048 | bytes 8760064 | tf_op jit(solution)/shard_map/add | solution.py:117
  70.2 0.0 copy-start
  70.3 4.6 %collective-permute-start.10 = (f32[2,128,128]{2,1,0:T(8,128)S(1)}, f32[2,128,128]{2,1,0:T(8,128)S(1)}, u32[]{:S(2)}, u32[]{:S(2)}) collective-permute-start(f32[2,128,128]{2,1,0:T(8,128)S(1)} %get-tuple-element.28), channel_id=1, source_target_pairs={{0,4},{4,8},{8,12},{1,5},{5,9},{9,13},{2,6},{6,10},{10,14},{3,7},{... | collective-permute-start | bytes 393224 | tf_op jit(solution)/shard_map/ppermute | solution.py:20
  74.8 1.3 %collective-permute-start.11 = (f32[2,128,128]{2,1,0:T(8,128)S(1)}, f32[2,128,128]{2,1,0:T(8,128)S(1)}, u32[]{:S(2)}, u32[]{:S(2)}) collective-permute-start(f32[2,128,128]{2,1,0:T(8,128)S(1)} %get-tuple-element.29), channel_id=1, source_target_pairs={{4,0},{8,4},{12,8},{5,1},{9,5},{13,9},{6,2},{10,6},{14,10},{7,3},{... | collective-permute-start | bytes 393224 | tf_op jit(solution)/shard_map/ppermute | solution.py:23
  76.2 0.1 fusion.73
  76.3 5.1 %collective-permute-start.18 = (f32[3,20,2]{2,1,0:T(8,128)S(1)}, f32[3,20,2]{2,1,0:T(8,128)S(1)}, u32[]{:S(2)}, u32[]{:S(2)}) collective-permute-start(f32[3,20,2]{2,1,0:T(8,128)S(1)} %get-tuple-element.39), channel_id=1, source_target_pairs={{0,2},{1,3},{4,6},{5,7},{8,10},{9,11},{12,14},{13,15},{16,18},{17,... | collective-permute-start | bytes 1448 | tf_op jit(solution)/shard_map/ppermute | solution.py:20
  81.4 1.3 %collective-permute-start.19 = (f32[3,20,2]{2,1,0:T(8,128)S(1)}, f32[3,20,2]{2,1,0:T(8,128)S(1)}, u32[]{:S(2)}, u32[]{:S(2)}) collective-permute-start(f32[3,20,2]{2,1,0:T(8,128)S(1)} %get-tuple-element.40), channel_id=1, source_target_pairs={{2,0},{3,1},{6,4},{7,5},{10,8},{11,9},{14,12},{15,13},{18,16},{19,... | collective-permute-start | bytes 1448 | tf_op jit(solution)/shard_map/ppermute | solution.py:23
  82.8 4.5 %collective-permute-start.12 = (f32[20,2,128]{2,1,0:T(2,128)S(1)}, f32[20,2,128]{2,1,0:T(2,128)S(1)}, u32[]{:S(2)}, u32[]{:S(2)}) collective-permute-start(f32[20,2,128]{2,1,0:T(2,128)S(1)} %get-tuple-element.18), channel_id=1, source_target_pairs={{0,2},{1,3},{4,6},{5,7},{8,10},{9,11},{12,14},{13,15},{16,18},{17,... | collective-permute-start | bytes 61448 | tf_op jit(solution)/shard_map/ppermute | solution.py:20
  87.3 1.3 %collective-permute-start.13 = (f32[20,2,128]{2,1,0:T(2,128)S(1)}, f32[20,2,128]{2,1,0:T(2,128)S(1)}, u32[]{:S(2)}, u32[]{:S(2)}) collective-permute-start(f32[20,2,128]{2,1,0:T(2,128)S(1)} %get-tuple-element.19), channel_id=1, source_target_pairs={{2,0},{3,1},{6,4},{7,5},{10,8},{11,9},{14,12},{15,13},{18,16},{19,... | collective-permute-start | bytes 61448 | tf_op jit(solution)/shard_map/ppermute | solution.py:23
  88.7 0.7 maximum_maximum_fusion.2
  89.4 3.6 %collective-permute-done.13 = f32[20,2,128]{2,1,0:T(2,128)S(1)} collective-permute-done((f32[20,2,128]{2,1,0:T(2,128)S(1)}, f32[20,2,128]{2,1,0:T(2,128)S(1)}, u32[]{:S(2)}, u32[]{:S(2)}) %collective-permute-start.13) | collective-permute-done | bytes 20512 | tf_op jit(solution)/shard_map/ppermute | solution.py:23
  93.0 0.1 pad_maximum_fusion.2
  93.2 2.3 %copy.36 = f32[20,132,128]{1,0,2:T(8,128)} copy(f32[20,132,128]{2,1,0:T(8,128)S(1)} %pad_maximum_fusion.2) | data formatting | bytes 2703360 | tf_op jit(solution)/shard_map/concatenate | solution.py:24
  95.5 0.8 fusion.68
  96.3 1.3 %collective-permute-start.14 = (f32[20,132,2]{1,0,2:T(8,128)S(1)}, f32[20,132,2]{1,0,2:T(8,128)S(1)}, u32[]{:S(2)}, u32[]{:S(2)}) collective-permute-start(f32[20,132,2]{1,0,2:T(8,128)S(1)} %get-tuple-element.12), channel_id=1, source_target_pairs={{0,1},{2,3},{4,5},{6,7},{8,9},{10,11},{12,13},{14,15},{16,17},{18,... | collective-permute-start | bytes 63368 | tf_op jit(solution)/shard_map/ppermute | solution.py:20
  97.6 1.6 %collective-permute-start.15 = (f32[20,132,2]{1,0,2:T(8,128)S(1)}, f32[20,132,2]{1,0,2:T(8,128)S(1)}, u32[]{:S(2)}, u32[]{:S(2)}) collective-permute-start(f32[20,132,2]{1,0,2:T(8,128)S(1)} %get-tuple-element.13), channel_id=1, source_target_pairs={{1,0},{3,2},{5,4},{7,6},{9,8},{11,10},{13,12},{15,14},{17,16},{19,... | collective-permute-start | bytes 63368 | tf_op jit(solution)/shard_map/ppermute | solution.py:23
  99.2 2.4 %maximum_maximum_fusion = (f32[20,130,128]{2,1,0:T(8,128)S(1)}, f32[20,130,128]{2,1,0:T(8,128)}) fusion(f32[2,128,128]{2,1,0:T(8,128)} %copy-done.9, f32[16,128,128]{2,1,0:T(8,128)S(1)} %fusion.20, f32[2,128,128]{2,1,0:T(8,128)} %copy-done.8, f32[20,2,128]{2,1,0:T(2,128)S(1)} %collective-permute-done.12, f32[20,2,128]{2,1,0:T(2,128)S(1)} %collective-permute-done.13), kind=kLoop, calls=%fused_computation.5 | loop fusion | flops 1996800 | bytes 4014080 | tf_op jit(solution)/shard_map/concatenate | solution.py:24
  101.7 0.4 pad_maximum_fusion.3
  102.0 0.2 copy-done.11
  102.2 0.0 copy-done.12
  102.3 0.6 pad_maximum_fusion.36
  102.9 5.6 %psum.15 = f32[3,16,128]{2,1,0:T(8,128)} all-reduce(f32[3,16,128]{2,1,0:T(8,128)} %pad_maximum_fusion.36), channel_id=1, replica_groups=mesh['groups'=2,'air'=4,'plate'=2,'field'=2] {'field'}, use_global_device_ids=true, to_apply=%region_1.2 | all-reduce | flops 6144 | bytes 49152 | tf_op jit(solution)/shard_map/psum | solution.py:99
  108.5 1.9 %fusion.66 = (f32[3,16,128]{2,1,0:T(8,128)S(1)}, f32[3,16,128]{2,1,0:T(8,128)}) fusion(f32[3,16,128]{2,1,0:T(8,128)S(1)} %get-tuple-element.11, f32[3,16,128]{2,1,0:T(8,128)} %psum.15, f32[3,20,130]{2,1,0:T(8,128)} %get-tuple-element.44, f32[3,20,130]{2,1,0:T(8,128)} %get-tuple-element.43, f32[3,2,128]{2,1,0:T(2,128)S(1)} %copy-done.21, ...), kind=kLoop, calls=%fused_computation.177 | loop fusion | flops 178176 | bytes 326064 | tf_op jit(solution)/shard_map/sub | solution.py:107
  110.4 0.6 slice_bitcast_fusion.2
  111.0 2.4 %copy.37 = f32[20,132,2]{2,1,0:T(8,128)} copy(f32[20,132,2]{1,0,2:T(8,128)} %copy-done.11) | data formatting | bytes 42240 | tf_op jit(solution)/shard_map/ppermute | solution.py:20
  113.4 1.6 %copy.39 = f32[20,132,2]{2,1,0:T(8,128)} copy(f32[20,132,2]{1,0,2:T(8,128)S(1)} %copy-done.13) | data formatting | bytes 42240 | tf_op jit(solution)/shard_map/ppermute | solution.py:23
  115.0 8.6 %fusion.9 = f32[16,128,128]{2,1,0:T(8,128)} fusion(f32[16,128,128]{2,1,0:T(8,128)S(1)} %fusion.20, f32[2,128,128]{2,1,0:T(8,128)} %copy-done.9, f32[2,128,128]{2,1,0:T(8,128)} %copy-done.8, f32[20,132,2]{2,1,0:T(8,128)} %copy.39, f32[20,2,128]{2,1,0:T(2,128)} %copy-done.15, f32[20,2,128]{2,1,0:T(2,128)} %copy-done.14, f32[20,132,2]{2,1,0:T(8,128)} %copy.37, ...), kind=kLoop, calls=%fused_computation.25 | loop fusion | flops 13107200 | bytes 7711488 | tf_op jit(solution)/shard_map/add | solution.py:117
  (84 shorter events, 0.3 us)
Async XLA Ops:
  0.6 25.6 %copy-start.2 = (f32[16,128,128]{2,1,0:T(8,128)S(1)}, f32[16,128,128]{2,1,0:T(8,128)}, u32[]{:S(2)}) copy-start(f32[16,128,128]{2,1,0:T(8,128)} %param.8) | copy-start | bytes 3145732
  1.7 24.5 %collective-permute-start = (f32[2,128,128]{2,1,0:T(8,128)S(1)}, f32[2,128,128]{2,1,0:T(8,128)S(1)}, u32[]{:S(2)}, u32[]{:S(2)}) collective-permute-start(f32[2,128,128]{2,1,0:T(8,128)S(1)} %get-tuple-element.34), channel_id=1, source_target_pairs={{0,4},{4,8},{8,12},{1,5},{5,9},{9,13},{2,6},{6,10},{10,14},{3,7},{... | collective-permute-start | bytes 393224 | tf_op jit(solution)/shard_map/ppermute | solution.py:20
  6.7 19.9 %collective-permute-start.1 = (f32[2,128,128]{2,1,0:T(8,128)S(1)}, f32[2,128,128]{2,1,0:T(8,128)S(1)}, u32[]{:S(2)}, u32[]{:S(2)}) collective-permute-start(f32[2,128,128]{2,1,0:T(8,128)S(1)} %get-tuple-element.33), channel_id=1, source_target_pairs={{4,0},{8,4},{12,8},{5,1},{9,5},{13,9},{6,2},{10,6},{14,10},{7,3},{... | collective-permute-start | bytes 393224 | tf_op jit(solution)/shard_map/ppermute | solution.py:23
  9.6 40.4 %copy-start.22 = (pred[3,128]{1,0:T(4,128)(4,1)}, pred[3,128]{1,0:T(4,128)(4,1)S(1)}, u32[]{:S(2)}) copy-start(pred[3,128]{1,0:T(4,128)(4,1)S(1)} %compare_and_fusion) | copy-start | bytes 1156
  9.7 40.4 %copy-start.24 = (pred[3,16]{1,0:T(4,128)(4,1)}, pred[3,16]{1,0:T(4,128)(4,1)S(1)}, u32[]{:S(2)}) copy-start(pred[3,16]{1,0:T(4,128)(4,1)S(1)} %compare_and_fusion.1) | copy-start | bytes 148
  10.5 15.7 %collective-permute-start.6 = (f32[3,2,128]{2,1,0:T(2,128)S(1)}, f32[3,2,128]{2,1,0:T(2,128)S(1)}, u32[]{:S(2)}, u32[]{:S(2)}) collective-permute-start(f32[3,2,128]{2,1,0:T(2,128)S(1)} %get-tuple-element.55), channel_id=1, source_target_pairs={{0,4},{4,8},{8,12},{1,5},{5,9},{9,13},{2,6},{6,10},{10,14},{3,7},{... | collective-permute-start | bytes 9224 | tf_op jit(solution)/shard_map/ppermute | solution.py:20
  15.0 11.1 %collective-permute-start.7 = (f32[3,2,128]{2,1,0:T(2,128)S(1)}, f32[3,2,128]{2,1,0:T(2,128)S(1)}, u32[]{:S(2)}, u32[]{:S(2)}) collective-permute-start(f32[3,2,128]{2,1,0:T(2,128)S(1)} %get-tuple-element.56), channel_id=1, source_target_pairs={{4,0},{8,4},{12,8},{5,1},{9,5},{13,9},{6,2},{10,6},{14,10},{7,3},{... | collective-permute-start | bytes 9224 | tf_op jit(solution)/shard_map/ppermute | solution.py:23
  21.6 38.5 %copy-start.26 = (f32[128]{0:T(128)}, f32[128]{0:T(128)S(1)}, u32[]{:S(2)}) copy-start(f32[128]{0:T(128)S(1)} %get-tuple-element.64) | copy-start | bytes 1540
  21.6 38.5 %copy-start.27 = (f32[128]{0:T(128)}, f32[128]{0:T(128)S(1)}, u32[]{:S(2)}) copy-start(f32[128]{0:T(128)S(1)} %get-tuple-element.65) | copy-start | bytes 1540
  26.6 10.7 %copy-start.7 = (f32[18,128,128]{2,1,0:T(8,128)}, f32[18,128,128]{2,1,0:T(8,128)S(1)}, u32[]{:S(2)}) copy-start(f32[18,128,128]{2,1,0:T(8,128)S(1)} %get-tuple-element.30) | copy-start | bytes 3538948
  26.6 10.7 %copy-start.4 = (f32[18,128,128]{2,1,0:T(8,128)}, f32[18,128,128]{2,1,0:T(8,128)S(1)}, u32[]{:S(2)}) copy-start(f32[18,128,128]{2,1,0:T(8,128)S(1)} %get-tuple-element.37) | copy-start | bytes 3538948
  26.6 10.7 %copy-start.6 = (f32[20,128,128]{2,1,0:T(8,128)}, f32[20,128,128]{2,1,0:T(8,128)S(1)}, u32[]{:S(2)}) copy-start(f32[20,128,128]{2,1,0:T(8,128)S(1)} %get-tuple-element.38) | copy-start | bytes 3932164
  26.7 10.6 %collective-permute-start.2 = (f32[20,2,128]{2,1,0:T(2,128)S(1)}, f32[20,2,128]{2,1,0:T(2,128)S(1)}, u32[]{:S(2)}, u32[]{:S(2)}) collective-permute-start(f32[20,2,128]{2,1,0:T(2,128)S(1)} %get-tuple-element.20), channel_id=1, source_target_pairs={{0,2},{1,3},{4,6},{5,7},{8,10},{9,11},{12,14},{13,15},{16,18},{17,... | collective-permute-start | bytes 61448 | tf_op jit(solution)/shard_map/ppermute | solution.py:20
  30.1 7.2 %collective-permute-start.3 = (f32[20,2,128]{2,1,0:T(2,128)S(1)}, f32[20,2,128]{2,1,0:T(2,128)S(1)}, u32[]{:S(2)}, u32[]{:S(2)}) collective-permute-start(f32[20,2,128]{2,1,0:T(2,128)S(1)} %get-tuple-element.21), channel_id=1, source_target_pairs={{2,0},{3,1},{6,4},{7,5},{10,8},{11,9},{14,12},{15,13},{18,16},{19,... | collective-permute-start | bytes 61448 | tf_op jit(solution)/shard_map/ppermute | solution.py:23
  31.5 12.2 %collective-permute-start.8 = (f32[3,20,2]{2,1,0:T(8,128)S(1)}, f32[3,20,2]{2,1,0:T(8,128)S(1)}, u32[]{:S(2)}, u32[]{:S(2)}) collective-permute-start(f32[3,20,2]{2,1,0:T(8,128)S(1)} %get-tuple-element.41), channel_id=1, source_target_pairs={{0,2},{1,3},{4,6},{5,7},{8,10},{9,11},{12,14},{13,15},{16,18},{17,... | collective-permute-start | bytes 1448 | tf_op jit(solution)/shard_map/ppermute | solution.py:20
  36.0 8.3 %collective-permute-start.9 = (f32[3,20,2]{2,1,0:T(8,128)S(1)}, f32[3,20,2]{2,1,0:T(8,128)}, u32[]{:S(2)}, u32[]{:S(2)}) collective-permute-start(f32[3,20,2]{2,1,0:T(8,128)S(1)} %get-tuple-element.42), channel_id=1, source_target_pairs={{2,0},{3,1},{6,4},{7,5},{10,8},{11,9},{14,12},{15,13},{18,16},{19,... | collective-permute-start | bytes 1448 | tf_op jit(solution)/shard_map/ppermute | solution.py:23
  41.1 4.1 %collective-permute-start.4 = (f32[20,132,2]{1,0,2:T(8,128)S(1)}, f32[20,132,2]{1,0,2:T(8,128)S(1)}, u32[]{:S(2)}, u32[]{:S(2)}) collective-permute-start(f32[20,132,2]{1,0,2:T(8,128)S(1)} %get-tuple-element.14), channel_id=1, source_target_pairs={{0,1},{2,3},{4,5},{6,7},{8,9},{10,11},{12,13},{14,15},{16,17},{18,... | collective-permute-start | bytes 63368 | tf_op jit(solution)/shard_map/ppermute | solution.py:20
  42.4 3.1 %collective-permute-start.5 = (f32[20,132,2]{1,0,2:T(8,128)S(1)}, f32[20,132,2]{1,0,2:T(8,128)S(1)}, u32[]{:S(2)}, u32[]{:S(2)}) collective-permute-start(f32[20,132,2]{1,0,2:T(8,128)S(1)} %get-tuple-element.15), channel_id=1, source_target_pairs={{1,0},{3,2},{5,4},{7,6},{9,8},{11,10},{13,12},{15,14},{17,16},{19,... | collective-permute-start | bytes 63368 | tf_op jit(solution)/shard_map/ppermute | solution.py:23
  43.7 0.6 copy-start.17
  50.9 57.6 %copy-start.10 = (f32[3,16,128]{2,1,0:T(8,128)}, f32[3,16,128]{2,1,0:T(8,128)S(1)}, u32[]{:S(2)}) copy-start(f32[3,16,128]{2,1,0:T(8,128)S(1)} %get-tuple-element.11) | copy-start | bytes 73732
  50.9 25.2 %collective-permute-start.16 = (f32[3,2,128]{2,1,0:T(2,128)S(1)}, f32[3,2,128]{2,1,0:T(2,128)S(1)}, u32[]{:S(2)}, u32[]{:S(2)}) collective-permute-start(f32[3,2,128]{2,1,0:T(2,128)S(1)} %get-tuple-element.50), channel_id=1, source_target_pairs={{0,4},{4,8},{8,12},{1,5},{5,9},{9,13},{2,6},{6,10},{10,14},{3,7},{... | collective-permute-start | bytes 9224 | tf_op jit(solution)/shard_map/ppermute | solution.py:20
  55.5 20.7 %collective-permute-start.17 = (f32[3,2,128]{2,1,0:T(2,128)S(1)}, f32[3,2,128]{2,1,0:T(2,128)S(1)}, u32[]{:S(2)}, u32[]{:S(2)}) collective-permute-start(f32[3,2,128]{2,1,0:T(2,128)S(1)} %get-tuple-element.51), channel_id=1, source_target_pairs={{4,0},{8,4},{12,8},{5,1},{9,5},{13,9},{6,2},{10,6},{14,10},{7,3},{... | collective-permute-start | bytes 9224 | tf_op jit(solution)/shard_map/ppermute | solution.py:23
  56.8 3.3 %copy-start.3 = (f32[16,128,128]{2,1,0:T(8,128)S(1)}, f32[16,128,128]{2,1,0:T(8,128)}, u32[]{:S(2)}) copy-start(f32[16,128,128]{2,1,0:T(8,128)} %param.8) | copy-start | bytes 3145732
  56.8 3.3 %copy-start.5 = (f32[18,128,128]{2,1,0:T(8,128)S(1)}, f32[18,128,128]{2,1,0:T(8,128)}, u32[]{:S(2)}) copy-start(f32[18,128,128]{2,1,0:T(8,128)} %copy-done.4) | copy-start | bytes 3538948
  56.8 3.3 %copy-start.28 = (f32[128]{0:T(128)S(1)}, f32[128]{0:T(128)}, u32[]{:S(2)}) copy-start(f32[128]{0:T(128)} %fusion.65) | copy-start | bytes 1540
  70.2 44.8 %copy-start = (f32[16,128,128]{2,1,0:T(8,128)}, f32[16,128,128]{2,1,0:T(8,128)S(1)}, u32[]{:S(2)}) copy-start(f32[16,128,128]{2,1,0:T(8,128)S(1)} %fusion.20) | copy-start | bytes 3145732
  70.3 12.4 %collective-permute-start.10 = (f32[2,128,128]{2,1,0:T(8,128)S(1)}, f32[2,128,128]{2,1,0:T(8,128)S(1)}, u32[]{:S(2)}, u32[]{:S(2)}) collective-permute-start(f32[2,128,128]{2,1,0:T(8,128)S(1)} %get-tuple-element.28), channel_id=1, source_target_pairs={{0,4},{4,8},{8,12},{1,5},{5,9},{9,13},{2,6},{6,10},{10,14},{3,7},{... | collective-permute-start | bytes 393224 | tf_op jit(solution)/shard_map/ppermute | solution.py:20
  74.8 7.9 %collective-permute-start.11 = (f32[2,128,128]{2,1,0:T(8,128)S(1)}, f32[2,128,128]{2,1,0:T(8,128)S(1)}, u32[]{:S(2)}, u32[]{:S(2)}) collective-permute-start(f32[2,128,128]{2,1,0:T(8,128)S(1)} %get-tuple-element.29), channel_id=1, source_target_pairs={{4,0},{8,4},{12,8},{5,1},{9,5},{13,9},{6,2},{10,6},{14,10},{7,3},{... | collective-permute-start | bytes 393224 | tf_op jit(solution)/shard_map/ppermute | solution.py:23
  76.1 13.2 %copy-start.18 = (f32[3,2,128]{2,1,0:T(2,128)}, f32[3,2,128]{2,1,0:T(2,128)S(1)}, u32[]{:S(2)}) copy-start(f32[3,2,128]{2,1,0:T(2,128)S(1)} %collective-permute-done.16) | copy-start | bytes 9220
  76.2 13.2 %copy-start.20 = (f32[3,2,128]{2,1,0:T(2,128)}, f32[3,2,128]{2,1,0:T(2,128)S(1)}, u32[]{:S(2)}) copy-start(f32[3,2,128]{2,1,0:T(2,128)S(1)} %collective-permute-done.17) | copy-start | bytes 9220
  76.3 12.4 %collective-permute-start.18 = (f32[3,20,2]{2,1,0:T(8,128)S(1)}, f32[3,20,2]{2,1,0:T(8,128)S(1)}, u32[]{:S(2)}, u32[]{:S(2)}) collective-permute-start(f32[3,20,2]{2,1,0:T(8,128)S(1)} %get-tuple-element.39), channel_id=1, source_target_pairs={{0,2},{1,3},{4,6},{5,7},{8,10},{9,11},{12,14},{13,15},{16,18},{17,... | collective-permute-start | bytes 1448 | tf_op jit(solution)/shard_map/ppermute | solution.py:20
  81.4 7.2 %collective-permute-start.19 = (f32[3,20,2]{2,1,0:T(8,128)S(1)}, f32[3,20,2]{2,1,0:T(8,128)S(1)}, u32[]{:S(2)}, u32[]{:S(2)}) collective-permute-start(f32[3,20,2]{2,1,0:T(8,128)S(1)} %get-tuple-element.40), channel_id=1, source_target_pairs={{2,0},{3,1},{6,4},{7,5},{10,8},{11,9},{14,12},{15,13},{18,16},{19,... | collective-permute-start | bytes 1448 | tf_op jit(solution)/shard_map/ppermute | solution.py:23
  82.7 10.3 %copy-start.8 = (f32[2,128,128]{2,1,0:T(8,128)}, f32[2,128,128]{2,1,0:T(8,128)S(1)}, u32[]{:S(2)}) copy-start(f32[2,128,128]{2,1,0:T(8,128)S(1)} %collective-permute-done.10) | copy-start | bytes 393220
  82.7 10.3 %copy-start.9 = (f32[2,128,128]{2,1,0:T(8,128)}, f32[2,128,128]{2,1,0:T(8,128)S(1)}, u32[]{:S(2)}) copy-start(f32[2,128,128]{2,1,0:T(8,128)S(1)} %collective-permute-done.11) | copy-start | bytes 393220
  82.8 6.6 %collective-permute-start.12 = (f32[20,2,128]{2,1,0:T(2,128)S(1)}, f32[20,2,128]{2,1,0:T(2,128)S(1)}, u32[]{:S(2)}, u32[]{:S(2)}) collective-permute-start(f32[20,2,128]{2,1,0:T(2,128)S(1)} %get-tuple-element.18), channel_id=1, source_target_pairs={{0,2},{1,3},{4,6},{5,7},{8,10},{9,11},{12,14},{13,15},{16,18},{17,... | collective-permute-start | bytes 61448 | tf_op jit(solution)/shard_map/ppermute | solution.py:20
  87.3 5.7 %collective-permute-start.13 = (f32[20,2,128]{2,1,0:T(2,128)S(1)}, f32[20,2,128]{2,1,0:T(2,128)S(1)}, u32[]{:S(2)}, u32[]{:S(2)}) collective-permute-start(f32[20,2,128]{2,1,0:T(2,128)S(1)} %get-tuple-element.19), channel_id=1, source_target_pairs={{2,0},{3,1},{6,4},{7,5},{10,8},{11,9},{14,12},{15,13},{18,16},{19,... | collective-permute-start | bytes 61448 | tf_op jit(solution)/shard_map/ppermute | solution.py:23
  89.4 9.8 %copy-start.14 = (f32[20,2,128]{2,1,0:T(2,128)}, f32[20,2,128]{2,1,0:T(2,128)S(1)}, u32[]{:S(2)}) copy-start(f32[20,2,128]{2,1,0:T(2,128)S(1)} %collective-permute-done.12) | copy-start | bytes 61444
  93.0 6.2 %copy-start.15 = (f32[20,2,128]{2,1,0:T(2,128)}, f32[20,2,128]{2,1,0:T(2,128)S(1)}, u32[]{:S(2)}) copy-start(f32[20,2,128]{2,1,0:T(2,128)S(1)} %collective-permute-done.13) | copy-start | bytes 61444
  96.3 5.3 %collective-permute-start.14 = (f32[20,132,2]{1,0,2:T(8,128)S(1)}, f32[20,132,2]{1,0,2:T(8,128)S(1)}, u32[]{:S(2)}, u32[]{:S(2)}) collective-permute-start(f32[20,132,2]{1,0,2:T(8,128)S(1)} %get-tuple-element.12), channel_id=1, source_target_pairs={{0,1},{2,3},{4,5},{6,7},{8,9},{10,11},{12,13},{14,15},{16,17},{18,... | collective-permute-start | bytes 63368 | tf_op jit(solution)/shard_map/ppermute | solution.py:20
  97.6 4.1 %copy-start.1 = (f32[20,132,128]{1,0,2:T(8,128)S(1)}, f32[20,132,128]{1,0,2:T(8,128)}, u32[]{:S(2)}) copy-start(f32[20,132,128]{1,0,2:T(8,128)} %copy.36) | copy-start | bytes 4055044
  97.6 4.0 %collective-permute-start.15 = (f32[20,132,2]{1,0,2:T(8,128)S(1)}, f32[20,132,2]{1,0,2:T(8,128)S(1)}, u32[]{:S(2)}, u32[]{:S(2)}) collective-permute-start(f32[20,132,2]{1,0,2:T(8,128)S(1)} %get-tuple-element.13), channel_id=1, source_target_pairs={{1,0},{3,2},{5,4},{7,6},{9,8},{11,10},{13,12},{15,14},{17,16},{19,... | collective-permute-start | bytes 63368 | tf_op jit(solution)/shard_map/ppermute | solution.py:23
  101.6 6.9 %copy-start.16 = (f32[3,16,128]{2,1,0:T(8,128)S(1)}, f32[3,16,128]{2,1,0:T(8,128)}, u32[]{:S(2)}) copy-start(f32[3,16,128]{2,1,0:T(8,128)} %param.10) | copy-start | bytes 73732
  101.6 6.9 %copy-start.19 = (f32[3,2,128]{2,1,0:T(2,128)S(1)}, f32[3,2,128]{2,1,0:T(2,128)}, u32[]{:S(2)}) copy-start(f32[3,2,128]{2,1,0:T(2,128)} %copy-done.18) | copy-start | bytes 9220
  101.6 6.9 %copy-start.21 = (f32[3,2,128]{2,1,0:T(2,128)S(1)}, f32[3,2,128]{2,1,0:T(2,128)}, u32[]{:S(2)}) copy-start(f32[3,2,128]{2,1,0:T(2,128)} %copy-done.20) | copy-start | bytes 9220
  101.6 6.9 %copy-start.23 = (pred[3,128]{1,0:T(4,128)(4,1)S(1)}, pred[3,128]{1,0:T(4,128)(4,1)}, u32[]{:S(2)}) copy-start(pred[3,128]{1,0:T(4,128)(4,1)} %copy-done.22) | copy-start | bytes 1156
  101.6 6.9 %copy-start.25 = (pred[3,16]{1,0:T(4,128)(4,1)S(1)}, pred[3,16]{1,0:T(4,128)(4,1)}, u32[]{:S(2)}) copy-start(pred[3,16]{1,0:T(4,128)(4,1)} %copy-done.24) | copy-start | bytes 148
  101.6 0.6 copy-start.11
  101.7 0.6 copy-start.12
  110.4 3.0 %copy-start.13 = (f32[20,132,2]{1,0,2:T(8,128)S(1)}, f32[20,132,2]{1,0,2:T(8,128)}, u32[]{:S(2)}) copy-start(f32[20,132,2]{1,0,2:T(8,128)} %copy-done.12) | copy-start | bytes 63364
where the time goes:
time: 125 us; the launch traced here: 124 us
  starting transfers between devices  51.9 us (42%)
  other arithmetic  29.8 us (24%)
  local copies, waits for them, and re-layouts  19 us (15%)
  blocking collectives  9.66 us (8%)
  between operations  9.21 us (7%)
  waiting for transfers between devices  3.93 us (3%)
    ppermute x10, starting transfers between devices, padded_2(): lax.ppermute(lax.slice_in_dim(block, block.shape[dim] - width, None, axis...  38.8 us
    add x2, other arithmetic, advance(): air_next = air_next + air_drive * source  18.7 us
    ppermute x10, starting transfers between devices, padded_2(): lax.ppermute(lax.slice_in_dim(block, 0, width, axis=dim), axis, backward)  13.2 us
    psum x2, blocking collectives, advance(): jump = lax.psum(local_jump, 'field')  9.66 us
    concatenate x9, other arithmetic, padded_2(): block = jnp.concatenate([low, block, high], axis=dim)  6.12 us
    concatenate x4, local copies, waits for them, and re-layouts, padded_2(): block = jnp.concatenate([low, block, high], axis=dim)  5.18 us
    ppermute x2, local copies, waits for them, and re-layouts, padded_2(): lax.ppermute(lax.slice_in_dim(block, block.shape[dim] - width, None, axis...  4.03 us
    ppermute x10, waiting for transfers between devices, padded_2(): lax.ppermute(lax.slice_in_dim(block, 0, width, axis=dim), axis, backward)  3.91 us
  transfers between devices with their start and end apart: 20, of which 2 were waited for; matrix products, arithmetic and copies ran while one was open for 21% of the time, Pallas kernels for 0%

commit v1 on v0

v1 whole, which is shorter than its diff:
```python
import functools

import jax
import jax.numpy as jnp
from jax import lax
from jax.experimental import pallas as pl
from jax.experimental.pallas import tpu as pltpu
from jax.sharding import PartitionSpec as P

F32 = jnp.float32
BF16 = jnp.bfloat16
MESH = pl.DeviceIdType.MESH
plate_step = 0.05
plate_load = 0.3
PAD = 8


def split_cat(value, axis):
    high = value.astype(BF16)
    low = (value - high.astype(F32)).astype(BF16)
    if axis == 0:
        return jnp.concatenate([high.astype(F32), low.astype(F32)], axis=0).astype(BF16)
    return jnp.concatenate([high, low], axis=1)


def kernel(
    counts,
    air_prev, air_now, plate_prev, plate_now, height, rows, cols,
    out_after, out_before, out_plate_after, out_plate_before,
    p0, p1, p2, p3, mx, sel_1, sel_1_in, sel_2, sel_2_in, drive,
    u0, u1, u1l, u1r, u2, u2l, u2r, u3,
    band, pick, weights,
    local_sem, send_sem, recv_sem,
):
    n_air, n_plate = counts
    nx, ny, nz = p0.shape
    plates = u0.shape[0]
    air, plate, field = lax.axis_index("air"), lax.axis_index("plate"), lax.axis_index("field")
    has = {
        "al": air > 0, "ah": air < n_air - 1,
        "pl": plate > 0, "ph": plate < n_plate - 1,
    }
    for a in ("al", "ah"):
        for b in ("pl", "ph"):
            has[a + b] = jnp.logical_and(has[a], has[b])
    has["f"] = None
    where = {
        "al": {"air": air - 1}, "ah": {"air": air + 1},
        "pl": {"plate": plate - 1}, "ph": {"plate": plate + 1},
        "alpl": {"air": air - 1, "plate": plate - 1}, "alph": {"air": air - 1, "plate": plate + 1},
        "ahpl": {"air": air + 1, "plate": plate - 1}, "ahph": {"air": air + 1, "plate": plate + 1},
        "f": {"field": 1 - field},
    }
    swap = {"al": "ah", "ah": "al", "pl": "ph", "ph": "pl", "": "", "f": "f"}

    def opposite(side):
        return swap[side[:2]] + swap[side[2:]]

    def when(cond, fn):
        if cond is None:
            fn()
        else:
            pl.when(cond)(fn)

    made = []

    def remote(side, src, dst):
        number = len(made)
        copy = pltpu.make_async_remote_copy(
            src_ref=src, dst_ref=dst,
            send_sem=send_sem.at[number], recv_sem=recv_sem.at[number],
            device_id=where[side], device_id_type=MESH,
        )
        made.append((side, copy))
        return number

    def start(number):
        side, copy = made[number]
        when(has[side], lambda: copy.start())

    def arrive(number):
        side, copy = made[number]
        when(has[opposite(side)], lambda: copy.wait_recv())

    def sent(number):
        side, copy = made[number]
        when(has[side], lambda: copy.wait_send())

    loads = [
        pltpu.make_async_copy(air_now, p1.at[pl.ds(2, nx), pl.ds(PAD, ny)], local_sem.at[0]),
        pltpu.make_async_copy(air_prev, p0, local_sem.at[1]),
        pltpu.make_async_copy(plate_now, u1.at[:, pl.ds(8, nx)], local_sem.at[2]),
        pltpu.make_async_copy(plate_prev, u0, local_sem.at[3]),
    ]
    for copy in loads:
        copy.start()

    barrier = pltpu.get_barrier_semaphore()
    total = jnp.int32(0)
    for side, target in where.items():
        def hail(target=target):
            pl.semaphore_signal(barrier, inc=1, device_id=target, device_id_type=MESH)
        when(has[side], hail)
        total = total + (1 if has[side] is None else has[side].astype(jnp.int32))
    pl.semaphore_wait(barrier, total)

    lo8, hi8 = pl.ds(0, 8), pl.ds(nx - 8, 8)
    own = pl.ds(8, nx)

    def plate_sends(src_own, src_lo, src_hi, mid, left, right):
        return [
            remote("al", src_lo, mid.at[:, pl.ds(8 + nx, 8)]),
            remote("ah", src_hi, mid.at[:, pl.ds(0, 8)]),
            remote("pl", src_own, right.at[:, own]),
            remote("ph", src_own, left.at[:, own]),
            remote("alpl", src_lo, right.at[:, pl.ds(8 + nx, 8)]),
            remote("alph", src_lo, left.at[:, pl.ds(8 + nx, 8)]),
            remote("ahpl", src_hi, right.at[:, pl.ds(0, 8)]),
            remote("ahph", src_hi, left.at[:, pl.ds(0, 8)]),
        ]

    def layer_send(src_ref, src_index, y_at, side, slot, dst):
        return remote(
            side,
            src_ref.at[pl.ds(src_index, 1), pl.ds(y_at, ny)],
            dst.at[pl.ds(slot, 1), pl.ds(PAD, ny)],
        )

    plates_1 = plate_sends(plate_now, plate_now.at[:, lo8], plate_now.at[:, hi8], u1, u1l, u1r)
    for number in plates_1:
        start(number)
    near_1 = [
        layer_send(air_now, 0, 0, "al", nx + 2, p1),
        layer_send(air_now, nx - 1, 0, "ah", 1, p1),
    ]
    far_1 = [
        layer_send(air_now, 1, 0, "al", nx + 3, p1),
        layer_send(air_now, nx - 2, 0, "ah", 0, p1),
    ]
    cols_1 = [
        remote("pl", air_now.at[:, pl.ds(0, 8)], p1.at[pl.ds(2, nx), pl.ds(PAD + ny, 8)]),
        remote("ph", air_now.at[:, pl.ds(ny - 8, 8)], p1.at[pl.ds(2, nx), pl.ds(0, 8)]),
    ]
    for number in near_1 + cols_1 + far_1:
        start(number)

    depth_start = field * nz
    lane8 = lax.broadcasted_iota(jnp.int32, (8, nz), 1)
    row8 = lax.broadcasted_iota(jnp.int32, (8, nz), 0)
    profile = jnp.zeros((8, nz), F32)
    for k in range(plates):
        at = lane8 + (depth_start - height[k])
        step = jnp.where(at == 1, 1.0, 0.0) - jnp.where(at == -1, 1.0, 0.0)
        profile = jnp.where(row8 == k, step, profile)
    low_field = field == 0
    edge = jnp.where(low_field, nz - 2, 0) + (row8 - plates)
    is_edge = jnp.logical_and(row8 >= plates, row8 < plates + 2)
    picks = jnp.where(jnp.logical_and(is_edge, lane8 == edge), 1.0, profile)
    picks = jnp.concatenate([picks, jnp.zeros((8, nz), F32)], axis=0).astype(BF16)
    pick[...] = jnp.concatenate([picks, picks], axis=1)
    halo_lane = jnp.where(low_field, nz, -2) + (row8 - plates)
    gap = jnp.abs(lane8 - halo_lane)
    halo_weight = jnp.where(gap == 1, 16.0, jnp.where(gap == 2, -1.0, 0.0))
    wts = jnp.where(is_edge, halo_weight, 6.0 * profile)
    weights[...] = jnp.concatenate([wts, wts], axis=0).astype(BF16)
    gap = jnp.abs(
        lax.broadcasted_iota(jnp.int32, (nz, nz), 0) - lax.broadcasted_iota(jnp.int32, (nz, nz), 1)
    )
    one = jnp.where(
        gap == 0, 30.0, jnp.where(gap == 1, 16.0, jnp.where(gap == 2, -1.0, 0.0))
    ).astype(BF16)
    band[pl.ds(0, nz), :] = one
    band[pl.ds(nz, nz), :] = one
    drive[...] = jnp.zeros(drive.shape, F32)

    def clear(ref):
        def rows_low():
            ref[pl.ds(0, 2), pl.ds(PAD, ny), :] = jnp.zeros((2, ny, nz), F32)
        def rows_high():
            ref[pl.ds(nx + 2, 2), pl.ds(PAD, ny), :] = jnp.zeros((2, ny, nz), F32)
        def cols_low():
            ref[pl.ds(2, nx), pl.ds(0, 8), :] = jnp.zeros((nx, 8, nz), F32)
        def cols_high():
            ref[pl.ds(2, nx), pl.ds(PAD + ny, 8), :] = jnp.zeros((nx, 8, nz), F32)
        pl.when(jnp.logical_not(has["al"]))(rows_low)
        pl.when(jnp.logical_not(has["ah"]))(rows_high)
        pl.when(jnp.logical_not(has["pl"]))(cols_low)
        pl.when(jnp.logical_not(has["ph"]))(cols_high)

    clear(p1)
    clear(p2)

    def prepare(value, x, sel):
        pieces = split_cat(value, 1)
        mx[x] = jnp.dot(pieces, band[...], preferred_element_type=F32)
        chosen = lax.dot_general(
            pick[...], pieces, (((1,), (1,)), ((), ())), preferred_element_type=F32
        )
        sel[pl.ds(pl.multiple_of(x * 8, 8), 8), :] = chosen[:8]

    def advance(now, back, x):
        nearest = (now[x + 1, pl.ds(PAD, ny), :] + now[x + 3, pl.ds(PAD, ny), :]) + (
            now[x + 2, pl.ds(PAD - 1, ny), :] + now[x + 2, pl.ds(PAD + 1, ny), :]
        )
        farther = (now[x, pl.ds(PAD, ny), :] + now[x + 4, pl.ds(PAD, ny), :]) + (
            now[x + 2, pl.ds(PAD - 2, ny), :] + now[x + 2, pl.ds(PAD + 2, ny), :]
        )
        pushed = lax.dot_general(
            split_cat(drive[pl.ds(pl.multiple_of(x * 8, 8), 8), :], 0), weights[...],
            (((0,), (0,)), ((), ())), preferred_element_type=F32,
        )
        return ((16.0 * nearest - farther) + (mx[x] + pushed)) * (1.0 / 60.0) - back

    row_at = lax.broadcasted_iota(jnp.int32, (nx + 16, ny), 0) + (air * nx - 8)
    lane_at = lax.broadcasted_iota(jnp.int32, (nx + 16, ny), 1)
    col_at = lane_at + plate * ny

    def plate_update(mid, left, right, back_of, sel, sel_in, k):
        inside_rows = jnp.logical_and(row_at >= rows[k, 0], row_at < rows[k, 1])

        def masked(value, shift):
            c = col_at + shift
            inside = jnp.logical_and(c >= cols[k, 0], c < cols[k, 1])
            return jnp.where(jnp.logical_and(inside_rows, inside), value, 0.0)

        c = masked(mid[k], 0)
        lft = masked(left[k], -ny)
        rgt = masked(right[k], ny)
        ym1 = pltpu.roll(jnp.where(lane_at >= ny - 1, lft, c), 1, 1)
        ym2 = pltpu.roll(jnp.where(lane_at >= ny - 2, lft, c), 2, 1)
        yp1 = pltpu.roll(jnp.where(lane_at < 1, rgt, c), ny - 1, 1)
        yp2 = pltpu.roll(jnp.where(lane_at < 2, rgt, c), ny - 2, 1)
        around = ym1 + yp1
        beside = 2.0 * around - 8.0 * c
        total = nx + 16
        bih = (
            (20.0 * c - 8.0 * around + (ym2 + yp2))
            + (pltpu.roll(beside, 1, 0) + pltpu.roll(beside, total - 1, 0))
            + (pltpu.roll(c, 2, 0) + pltpu.roll(c, total - 2, 0))
        )[8 : 8 + nx]
        centre = c[8 : 8 + nx]
        mask = masked(jnp.ones((nx + 16, ny), F32), 0)[8 : 8 + nx]
        jump = sel[pl.ds(k, nx, stride=8), :] + sel_in[pl.ds(k, nx, stride=8), :]
        after = mask * (2.0 * centre - back_of(k, mask) - plate_step * bih - plate_load * jump)
        drive[pl.ds(k, nx, stride=8), :] = after - centre
        return after

    def take_edges(sel_in):
        for j in range(2):
            drive[pl.ds(plates + j, nx, stride=8), :] = sel_in[pl.ds(plates + j, nx, stride=8), :]

    loads[0].wait()

    @pl.loop(0, nx)
    def _(x):
        prepare(p1[x + 2, pl.ds(PAD, ny), :], x, sel_1)

    swap_1 = remote("f", sel_1, sel_1_in)
    start(swap_1)
    for copy in loads[1:]:
        copy.wait()
    for number in plates_1:
        arrive(number)
    arrive(swap_1)
    for k in range(plates):
        u2[k, own, :] = plate_update(
            u1, u1l, u1r, lambda k, mask: mask * u0[k], sel_1, sel_1_in, k
        )
    take_edges(sel_1_in)
    plates_2 = plate_sends(u2.at[:, own], u2.at[:, pl.ds(8, 8)], u2.at[:, pl.ds(nx, 8)], u2, u2l, u2r)
    for number in plates_2:
        start(number)
    for number in cols_1:
        arrive(number)

    def first(x):
        value = advance(p1, p0[x], x)
        p2[x + 2, pl.ds(PAD, ny), :] = value
        prepare(value, x, sel_2)

    arrive(near_1[1])
    first(1)
    far_low = layer_send(p2, 3, PAD, "al", nx + 3, p2)
    start(far_low)
    arrive(near_1[0])
    first(nx - 2)
    far_high = layer_send(p2, nx, PAD, "ah", 0, p2)
    start(far_high)

    @pl.loop(2, nx - 2)
    def _(x):
        first(x)

    arrive(far_1[1])
    first(0)
    near_low = layer_send(p2, 2, PAD, "al", nx + 2, p2)
    start(near_low)
    arrive(far_1[0])
    first(nx - 1)
    near_high = layer_send(p2, nx + 1, PAD, "ah", 1, p2)
    start(near_high)
    swap_2 = remote("f", sel_2, sel_2_in)
    start(swap_2)
    cols_2 = [
        remote("pl", p2.at[pl.ds(2, nx), pl.ds(PAD, 8)], p2.at[pl.ds(2, nx), pl.ds(PAD + ny, 8)]),
        remote("ph", p2.at[pl.ds(2, nx), pl.ds(ny, 8)], p2.at[pl.ds(2, nx), pl.ds(0, 8)]),
    ]
    for number in cols_2:
        start(number)
    stores = [
        pltpu.make_async_copy(p2.at[pl.ds(2, nx), pl.ds(PAD, ny)], out_before, local_sem.at[0]),
        pltpu.make_async_copy(u2.at[:, own], out_plate_before, local_sem.at[1]),
    ]
    for copy in stores:
        copy.start()

    for number in plates_2:
        arrive(number)
    arrive(swap_2)
    for k in range(plates):
        u3[k] = plate_update(
            u2, u2l, u2r, lambda k, mask: mask * u1[k, own, :], sel_2, sel_2_in, k
        )
    take_edges(sel_2_in)
    stores.append(pltpu.make_async_copy(u3, out_plate_after, local_sem.at[2]))
    stores[-1].start()
    for number in cols_2:
        arrive(number)

    def second(x):
        p3[x] = advance(p2, p1[x + 2, pl.ds(PAD, ny), :], x)

    @pl.loop(2, nx - 2)
    def _(x):
        second(x)

    stores.append(
        pltpu.make_async_copy(
            p3.at[pl.ds(2, nx - 4)], out_after.at[pl.ds(2, nx - 4)], local_sem.at[3]
        )
    )
    stores[-1].start()
    arrive(far_high)
    arrive(near_high)
    second(0)
    second(1)
    stores.append(pltpu.make_async_copy(p3.at[pl.ds(0, 2)], out_after.at[pl.ds(0, 2)], local_sem.at[4]))
    stores[-1].start()
    arrive(far_low)
    arrive(near_low)
    second(nx - 2)
    second(nx - 1)
    stores.append(
        pltpu.make_async_copy(
            p3.at[pl.ds(nx - 2, 2)], out_after.at[pl.ds(nx - 2, 2)], local_sem.at[5]
        )
    )
    stores[-1].start()
    for number in range(len(made)):
        sent(number)
    for copy in stores:
        copy.wait()


REMOTES = 30


def on_device(counts, *arrays):
    air_prev, _, plate_prev, _, _, _, _ = arrays
    nx, ny, nz = air_prev.shape
    plates = plate_prev.shape[0]
    padded = pltpu.VMEM((nx + 4, ny + 2 * PAD, nz), F32)
    block = pltpu.VMEM((nx, ny, nz), F32)
    flat = pltpu.VMEM((nx * 8, ny), F32)
    tall = pltpu.VMEM((plates, nx + 16, ny), F32)
    tile = pltpu.VMEM((plates, nx, ny), F32)
    anywhere = pl.BlockSpec(memory_space=pl.ANY)
    scalars = pl.BlockSpec(memory_space=pltpu.SMEM)
    air = jax.ShapeDtypeStruct(air_prev.shape, F32)
    plate = jax.ShapeDtypeStruct(plate_prev.shape, F32)
    return pl.pallas_call(
        functools.partial(kernel, counts),
        out_shape=(air, air, plate, plate),
        in_specs=[anywhere] * 4 + [scalars] * 3,
        out_specs=(anywhere,) * 4,
        scratch_shapes=[
            block, padded, padded, block, block, flat, flat, flat, flat, flat,
            tile, tall, tall, tall, tall, tall, tall, tile,
            pltpu.VMEM((2 * nz, nz), BF16),
            pltpu.VMEM((16, 2 * nz), BF16),
            pltpu.VMEM((16, nz), BF16),
            pltpu.SemaphoreType.DMA((6,)),
            pltpu.SemaphoreType.DMA((REMOTES,)),
            pltpu.SemaphoreType.DMA((REMOTES,)),
        ],
        compiler_params=pltpu.CompilerParams(
            collective_id=0, has_side_effects=True, vmem_limit_bytes=24 * 1024 * 1024
        ),
        cost_estimate=pl.CostEstimate(
            flops=50 * nx * ny * nz, bytes_accessed=16 * nx * ny * nz, transcendentals=0
        ),
    )(*arrays)


def solution(mesh):
    counts = (mesh.shape["air"], mesh.shape["plate"])
    air = P(("groups", "air"), "plate", "field")
    plate = P("groups", "air", "plate")
    return jax.shard_map(
        functools.partial(on_device, counts),
        mesh=mesh,
        in_specs=(air, air, plate, plate, P("groups"), P("groups", None), P("groups", None)),
        out_specs=(air, air, plate, plate),
        check_vma=False,
    )
```

time: 125 us -> 31.1 us (0.25)
  starting transfers between devices: 51.9 us -> 0 us
  other arithmetic: 29.8 us -> 0 us
  Pallas kernels: 0 us -> 21.6 us
  local copies, waits for them, and re-layouts: 19 us -> 8.51 us
  blocking collectives: 9.66 us -> 0 us
  between operations: 9.21 us -> 0.66 us
  waiting for transfers between devices: 3.93 us -> 0 us
    ppermute x20 -> x0, starting transfers between devices: 51.9 us -> none  [the longest x10 38.8 us: padded_2(): lax.ppermute(lax.slice_in_dim(block, block.shape[dim] - width, None, axis...]
    pallas_call x0 -> x1, Pallas kernels: none -> 21.6 us  [on_device(): pl.pallas_call(functools.partial(kernel, counts), out_shape=(air, air, pl...]
    add x4 -> x0, other arithmetic: 18.7 us -> none  [the longest x2 18.7 us: advance(): air_next = air_next + air_drive * source]
    psum x2 -> x0, blocking collectives: 9.66 us -> none  [advance(): jump = lax.psum(local_jump, 'field')]
    unnamed x59 -> x18, local copies, waits for them, and re-layouts: 1.01 us -> 8.51 us
    ppermute x4 -> x0, local copies, waits for them, and re-layouts: 7.26 us -> none  [the longest x2 4.03 us: padded_2(): lax.ppermute(lax.slice_in_dim(block, block.shape[dim] - width, None, axis...]
    concatenate x9 -> x0, other arithmetic: 6.12 us -> none  [padded_2(): block = jnp.concatenate([low, block, high], axis=dim)]
    concatenate x4 -> x0, local copies, waits for them, and re-layouts: 5.18 us -> none  [padded_2(): block = jnp.concatenate([low, block, high], axis=dim)]
  transfers between devices with their start and end apart: 20 -> 0, of which waited for: 2 -> 0; matrix products, arithmetic and copies ran while one was open for 21% -> 0% of each run, Pallas kernels for 0% -> 0%
where the time goes in v1:
time: 31.1 us; the launch traced here: 30.7 us
  Pallas kernels  21.6 us (69%)
  local copies, waits for them, and re-layouts  8.51 us (27%)
  between operations  0.66 us (2%)
    pallas_call x1, Pallas kernels, on_device(): pl.pallas_call(functools.partial(kernel, counts), out_shape=(air, air, pl...  21.6 us
    unnamed x18, local copies, waits for them, and re-layouts  8.51 us

profile of v1, /device:TPU:0, one launch (start us, length us, event | category | flops | bytes accessed | tf_op | source)
XLA Modules:
  0.0 30.7 jit_solution(10553347816405981466)
XLA Ops:
  0.6 0.0 copy-start.5
  0.6 0.8 %copy.11.rows = s32[3,2]{1,0:T(4,128)S(1)} copy(s32[3,2]{0,1:T(2,128)} %param.12) | data formatting | bytes 48 | tf_op args[5]
  1.4 0.0 copy-done.5
  1.4 0.0 copy-start.4
  1.4 0.1 copy.12.cols
  1.5 0.6 %copy-done.4 = s32[3]{0:T(128)S(1)} copy-done((s32[3]{0:T(128)S(1)}, s32[3]{0:T(128)}, u32[]{:S(2)}) %copy-start.4) | copy-done | bytes 36
  2.1 0.0 copy-start
  2.1 1.2 %copy-done = f32[16,128,128]{2,1,0:T(8,128)S(1)} copy-done((f32[16,128,128]{2,1,0:T(8,128)S(1)}, f32[16,128,128]{2,1,0:T(8,128)}, u32[]{:S(2)}) %copy-start) | copy-done | bytes 1048600
  3.3 0.0 copy-start.1
  3.3 1.2 %copy-done.1 = f32[16,128,128]{2,1,0:T(8,128)S(1)} copy-done((f32[16,128,128]{2,1,0:T(8,128)S(1)}, f32[16,128,128]{2,1,0:T(8,128)}, u32[]{:S(2)}) %copy-start.1) | copy-done | bytes 1048600
  4.5 0.0 copy-start.2
  4.5 0.7 %copy-done.2 = f32[3,16,128]{2,1,0:T(8,128)S(1)} copy-done((f32[3,16,128]{2,1,0:T(8,128)S(1)}, f32[3,16,128]{2,1,0:T(8,128)}, u32[]{:S(2)}) %copy-start.2) | copy-done | bytes 24600
  5.3 0.0 copy-start.3
  5.3 0.7 %copy-done.3 = f32[3,16,128]{2,1,0:T(8,128)S(1)} copy-done((f32[3,16,128]{2,1,0:T(8,128)S(1)}, f32[3,16,128]{2,1,0:T(8,128)}, u32[]{:S(2)}) %copy-start.3) | copy-done | bytes 24600
  6.0 21.6 %shard_map.102 = (f32[16,128,128]{2,1,0:T(8,128)S(1)}, f32[16,128,128]{2,1,0:T(8,128)S(1)}, f32[3,16,128]{2,1,0:T(8,128)S(1)}, f32[3,16,128]{2,1,0:T(8,128)S(1)}) custom-call(f32[16,128,128]{2,1,0:T(8,128)S(1)} %copy-done, f32[16,128,128]{2,1,0:T(8,128)S(1)} %copy-done.1, f32[3,16,128]{2,1,0:T(8,128)S(1)} %copy-done.2, f32[3,16,128]{2,1,0:T(8,128)S(1)} %copy-done.3, ...), custom_call_target="tpu_custom_call" | custom-call | flops 13107200 | bytes 4194304 | tf_op jit(solution)/shard_map/pallas_call | solution.py:381
  27.6 1.0 %copy.17 = f32[16,128,128]{2,1,0:T(8,128)} copy(f32[16,128,128]{2,1,0:T(8,128)S(1)} %get-tuple-element.8) | data formatting | bytes 2097152
  28.6 1.0 %copy.18 = f32[16,128,128]{2,1,0:T(8,128)} copy(f32[16,128,128]{2,1,0:T(8,128)S(1)} %get-tuple-element.9) | data formatting | bytes 2097152
  29.5 0.6 %copy.19 = f32[3,16,128]{2,1,0:T(8,128)} copy(f32[3,16,128]{2,1,0:T(8,128)S(1)} %get-tuple-element.10) | data formatting | bytes 49152
  30.1 0.6 %copy.20 = f32[3,16,128]{2,1,0:T(8,128)} copy(f32[3,16,128]{2,1,0:T(8,128)S(1)} %get-tuple-element.11) | data formatting | bytes 49152
Async XLA Ops:
  0.6 0.8 %copy-start.5 = (s32[3,2]{0,1:T(2,128)S(1)}, s32[3,2]{0,1:T(2,128)}, u32[]{:S(2)}) copy-start(s32[3,2]{0,1:T(2,128)} %param.13) | copy-start | bytes 76
  1.4 0.7 %copy-start.4 = (s32[3]{0:T(128)S(1)}, s32[3]{0:T(128)}, u32[]{:S(2)}) copy-start(s32[3]{0:T(128)} %height.1) | copy-start | bytes 40
  2.1 1.2 %copy-start = (f32[16,128,128]{2,1,0:T(8,128)S(1)}, f32[16,128,128]{2,1,0:T(8,128)}, u32[]{:S(2)}) copy-start(f32[16,128,128]{2,1,0:T(8,128)} %air_prev.1) | copy-start | bytes 3145732
  3.3 1.2 %copy-start.1 = (f32[16,128,128]{2,1,0:T(8,128)S(1)}, f32[16,128,128]{2,1,0:T(8,128)}, u32[]{:S(2)}) copy-start(f32[16,128,128]{2,1,0:T(8,128)} %air_now.1) | copy-start | bytes 3145732
  4.5 0.7 %copy-start.2 = (f32[3,16,128]{2,1,0:T(8,128)S(1)}, f32[3,16,128]{2,1,0:T(8,128)}, u32[]{:S(2)}) copy-start(f32[3,16,128]{2,1,0:T(8,128)} %plate_prev.1) | copy-start | bytes 73732
  5.3 0.7 %copy-start.3 = (f32[3,16,128]{2,1,0:T(8,128)S(1)}, f32[3,16,128]{2,1,0:T(8,128)}, u32[]{:S(2)}) copy-start(f32[3,16,128]{2,1,0:T(8,128)} %plate_now.1) | copy-start | bytes 73732

commit v2 on v1

--- a/solution.py
+++ b/solution.py
@@ -25,11 +25,11 @@
 
 def kernel(
     counts,
-    air_prev, air_now, plate_prev, plate_now, height, rows, cols,
+    air_prev, air_now, plate_prev, plate_now, height_in, rows_in, cols_in,
     out_after, out_before, out_plate_after, out_plate_before,
-    p0, p1, p2, p3, mx, sel_1, sel_1_in, sel_2, sel_2_in, drive,
-    u0, u1, u1l, u1r, u2, u2l, u2r, u3,
-    band, pick, weights,
+    p0, p1, p2, mx, sel_1, sel_1_in, sel_2, sel_2_in, drive,
+    u0, u1, u1l, u1r, u2, u2l, u2r,
+    band, pick, weights, height, rows, cols,
     local_sem, send_sem, recv_sem,
 ):
     n_air, n_plate = counts
@@ -91,6 +91,9 @@
         pltpu.make_async_copy(air_prev, p0, local_sem.at[1]),
         pltpu.make_async_copy(plate_now, u1.at[:, pl.ds(8, nx)], local_sem.at[2]),
         pltpu.make_async_copy(plate_prev, u0, local_sem.at[3]),
+        pltpu.make_async_copy(height_in, height, local_sem.at[4]),
+        pltpu.make_async_copy(rows_in, rows, local_sem.at[5]),
+        pltpu.make_async_copy(cols_in, cols, local_sem.at[6]),
     ]
     for copy in loads:
         copy.start()
@@ -144,6 +147,8 @@
     for number in near_1 + cols_1 + far_1:
         start(number)
 
+    for copy in loads[4:]:
+        copy.wait()
     depth_start = field * nz
     lane8 = lax.broadcasted_iota(jnp.int32, (8, nz), 1)
     row8 = lax.broadcasted_iota(jnp.int32, (8, nz), 0)
@@ -196,7 +201,7 @@
         chosen = lax.dot_general(
             pick[...], pieces, (((1,), (1,)), ((), ())), preferred_element_type=F32
         )
-        sel[pl.ds(pl.multiple_of(x * 8, 8), 8), :] = chosen[:8]
+        sel[pl.ds(x * 8, 8), :] = chosen[:8]
 
     def advance(now, back, x):
         nearest = (now[x + 1, pl.ds(PAD, ny), :] + now[x + 3, pl.ds(PAD, ny), :]) + (
@@ -206,7 +211,7 @@
             now[x + 2, pl.ds(PAD - 2, ny), :] + now[x + 2, pl.ds(PAD + 2, ny), :]
         )
         pushed = lax.dot_general(
-            split_cat(drive[pl.ds(pl.multiple_of(x * 8, 8), 8), :], 0), weights[...],
+            split_cat(drive[pl.ds(x * 8, 8), :], 0), weights[...],
             (((0,), (0,)), ((), ())), preferred_element_type=F32,
         )
         return ((16.0 * nearest - farther) + (mx[x] + pushed)) * (1.0 / 60.0) - back
@@ -216,11 +221,11 @@
     col_at = lane_at + plate * ny
 
     def plate_update(mid, left, right, back_of, sel, sel_in, k):
-        inside_rows = jnp.logical_and(row_at >= rows[k, 0], row_at < rows[k, 1])
+        inside_rows = jnp.logical_and(row_at >= rows[0, k], row_at < rows[1, k])
 
         def masked(value, shift):
             c = col_at + shift
-            inside = jnp.logical_and(c >= cols[k, 0], c < cols[k, 1])
+            inside = jnp.logical_and(c >= cols[0, k], c < cols[1, k])
             return jnp.where(jnp.logical_and(inside_rows, inside), value, 0.0)
 
         c = masked(mid[k], 0)
@@ -251,13 +256,12 @@
 
     loads[0].wait()
 
-    @pl.loop(0, nx)
-    def _(x):
+    for x in range(nx):
         prepare(p1[x + 2, pl.ds(PAD, ny), :], x, sel_1)
 
     swap_1 = remote("f", sel_1, sel_1_in)
     start(swap_1)
-    for copy in loads[1:]:
+    for copy in loads[1:4]:
         copy.wait()
     for number in plates_1:
         arrive(number)
@@ -287,8 +291,7 @@
     far_high = layer_send(p2, nx, PAD, "ah", 0, p2)
     start(far_high)
 
-    @pl.loop(2, nx - 2)
-    def _(x):
+    for x in range(2, nx - 2):
         first(x)
 
     arrive(far_1[1])
@@ -318,44 +321,27 @@
         arrive(number)
     arrive(swap_2)
     for k in range(plates):
-        u3[k] = plate_update(
+        out_plate_after[k] = plate_update(
             u2, u2l, u2r, lambda k, mask: mask * u1[k, own, :], sel_2, sel_2_in, k
         )
     take_edges(sel_2_in)
-    stores.append(pltpu.make_async_copy(u3, out_plate_after, local_sem.at[2]))
-    stores[-1].start()
     for number in cols_2:
         arrive(number)
 
     def second(x):
-        p3[x] = advance(p2, p1[x + 2, pl.ds(PAD, ny), :], x)
-
-    @pl.loop(2, nx - 2)
-    def _(x):
+        out_after[x] = advance(p2, p1[x + 2, pl.ds(PAD, ny), :], x)
+
+    for x in range(2, nx - 2):
         second(x)
 
-    stores.append(
-        pltpu.make_async_copy(
-            p3.at[pl.ds(2, nx - 4)], out_after.at[pl.ds(2, nx - 4)], local_sem.at[3]
-        )
-    )
-    stores[-1].start()
     arrive(far_high)
     arrive(near_high)
     second(0)
     second(1)
-    stores.append(pltpu.make_async_copy(p3.at[pl.ds(0, 2)], out_after.at[pl.ds(0, 2)], local_sem.at[4]))
-    stores[-1].start()
     arrive(far_low)
     arrive(near_low)
     second(nx - 2)
     second(nx - 1)
-    stores.append(
-        pltpu.make_async_copy(
-            p3.at[pl.ds(nx - 2, 2)], out_after.at[pl.ds(nx - 2, 2)], local_sem.at[5]
-        )
-    )
-    stores[-1].start()
     for number in range(len(made)):
         sent(number)
     for copy in stores:
@@ -363,6 +349,17 @@
 
 
 REMOTES = 30
+
+
+def put_kernel(*refs):
+    count = (len(refs) - 1) // 2
+    copies = [
+        pltpu.make_async_copy(refs[i], refs[count + i], refs[-1].at[i]) for i in range(count)
+    ]
+    for copy in copies:
+        copy.start()
+    for copy in copies:
+        copy.wait()
 
 
 def on_device(counts, *arrays):
@@ -375,31 +372,46 @@
     tall = pltpu.VMEM((plates, nx + 16, ny), F32)
     tile = pltpu.VMEM((plates, nx, ny), F32)
     anywhere = pl.BlockSpec(memory_space=pl.ANY)
-    scalars = pl.BlockSpec(memory_space=pltpu.SMEM)
+    stored = pl.BlockSpec(memory_space=pltpu.HBM)
     air = jax.ShapeDtypeStruct(air_prev.shape, F32)
     plate = jax.ShapeDtypeStruct(plate_prev.shape, F32)
-    return pl.pallas_call(
+    held_air = pltpu.VMEM(air.shape, F32)
+    held_plate = pltpu.VMEM(plate.shape, F32)
+    results = pl.pallas_call(
         functools.partial(kernel, counts),
-        out_shape=(air, air, plate, plate),
-        in_specs=[anywhere] * 4 + [scalars] * 3,
-        out_specs=(anywhere,) * 4,
+        out_shape=(held_air, held_air, held_plate, held_plate),
+        in_specs=[stored] * 7,
+        out_specs=(pl.BlockSpec(memory_space=pltpu.VMEM),) * 4,
         scratch_shapes=[
-            block, padded, padded, block, block, flat, flat, flat, flat, flat,
-            tile, tall, tall, tall, tall, tall, tall, tile,
+            block, padded, padded, block, flat, flat, flat, flat, flat,
+            tile, tall, tall, tall, tall, tall, tall,
             pltpu.VMEM((2 * nz, nz), BF16),
             pltpu.VMEM((16, 2 * nz), BF16),
             pltpu.VMEM((16, nz), BF16),
-            pltpu.SemaphoreType.DMA((6,)),
+            pltpu.SMEM((plates,), jnp.int32),
+            pltpu.SMEM((2, plates), jnp.int32),
+            pltpu.SMEM((2, plates), jnp.int32),
+            pltpu.SemaphoreType.DMA((7,)),
             pltpu.SemaphoreType.DMA((REMOTES,)),
             pltpu.SemaphoreType.DMA((REMOTES,)),
         ],
         compiler_params=pltpu.CompilerParams(
-            collective_id=0, has_side_effects=True, vmem_limit_bytes=24 * 1024 * 1024
+            collective_id=0, has_side_effects=True, vmem_limit_bytes=60 * 1024 * 1024
         ),
         cost_estimate=pl.CostEstimate(
             flops=50 * nx * ny * nz, bytes_accessed=16 * nx * ny * nz, transcendentals=0
         ),
-    )(*arrays)
+    )(*arrays[:5], arrays[5].T, arrays[6].T)
+    return pl.pallas_call(
+        put_kernel,
+        out_shape=(air, air, plate, plate),
+        in_specs=[pl.BlockSpec(memory_space=pltpu.VMEM)] * 4,
+        out_specs=(stored,) * 4,
+        scratch_shapes=[pltpu.SemaphoreType.DMA((4,))],
+        cost_estimate=pl.CostEstimate(
+            flops=0, bytes_accessed=16 * nx * ny * nz, transcendentals=0
+        ),
+    )(*[pltpu.with_memory_space_constraint(one, pltpu.VMEM) for one in results])
 
 
 def solution(mesh):

time: 31.1 us -> 19 us (0.61)
  local copies, waits for them, and re-layouts: 8.51 us -> 0 us
  Pallas kernels: 21.6 us -> 18.2 us
    unnamed x18 -> x0, local copies, waits for them, and re-layouts: 8.51 us -> none
    pallas_call x1 -> x2, Pallas kernels: 21.6 us -> 18.2 us  [the longest x1 16.8 us: on_device(): pl.pallas_call(functools.partial(kernel, counts), out_shape=(held_air, he...]
where the time goes in v2:
time: 19 us; the launch traced here: 18.8 us
  Pallas kernels  18.2 us (96%)
  between operations  0.64 us (3%)
    pallas_call x1, Pallas kernels, on_device(): pl.pallas_call(functools.partial(kernel, counts), out_shape=(held_air, he...  16.8 us
    pallas_call x1, Pallas kernels, on_device(): pl.pallas_call(put_kernel, out_shape=(air, air, plate, plate), in_specs=[...  1.36 us

profile of v2, /device:TPU:0, one launch (start us, length us, event | category | flops | bytes accessed | tf_op | source)
XLA Modules:
  0.0 18.8 jit_solution(3944706882936037358)
XLA Ops:
  0.6 16.8 %shard_map.102 = (f32[16,128,128]{2,1,0:T(8,128)S(1)}, f32[16,128,128]{2,1,0:T(8,128)S(1)}, f32[3,16,128]{2,1,0:T(8,128)S(1)}, f32[3,16,128]{2,1,0:T(8,128)S(1)}) custom-call(f32[16,128,128]{2,1,0:T(8,128)} %air_prev.1, f32[16,128,128]{2,1,0:T(8,128)} %air_now.1, f32[3,16,128]{2,1,0:T(8,128)} %plate_prev.1, f32[3,16,128]{2,1,0:T(8,128)} %plate_now.1, ...), custom_call_target="tpu_custom_call" | custom-call | flops 13107200 | bytes 4194304 | tf_op jit(solution)/shard_map/pallas_call | solution.py:380
  17.5 1.4 %shard_map.103 = (f32[16,128,128]{2,1,0:T(8,128)}, f32[16,128,128]{2,1,0:T(8,128)}, f32[3,16,128]{2,1,0:T(8,128)}, f32[3,16,128]{2,1,0:T(8,128)}) custom-call(f32[16,128,128]{2,1,0:T(8,128)S(1)} %get-tuple-element.8.refs_0_, f32[16,128,128]{2,1,0:T(8,128)S(1)} %get-tuple-element.9.refs_1_, f32[3,16,128]{2,1,0:T(8,128)S(1)} %get-tuple-element.10.refs_2_, ...), custom_call_target="tpu_custom_call" | custom-call | bytes 4194304 | tf_op jit(solution)/shard_map/pallas_call | solution.py:405

commit v3 on v2

--- a/solution.py
+++ b/solution.py
@@ -105,48 +105,6 @@
             pl.semaphore_signal(barrier, inc=1, device_id=target, device_id_type=MESH)
         when(has[side], hail)
         total = total + (1 if has[side] is None else has[side].astype(jnp.int32))
-    pl.semaphore_wait(barrier, total)
-
-    lo8, hi8 = pl.ds(0, 8), pl.ds(nx - 8, 8)
-    own = pl.ds(8, nx)
-
-    def plate_sends(src_own, src_lo, src_hi, mid, left, right):
-        return [
-            remote("al", src_lo, mid.at[:, pl.ds(8 + nx, 8)]),
-            remote("ah", src_hi, mid.at[:, pl.ds(0, 8)]),
-            remote("pl", src_own, right.at[:, own]),
-            remote("ph", src_own, left.at[:, own]),
-            remote("alpl", src_lo, right.at[:, pl.ds(8 + nx, 8)]),
-            remote("alph", src_lo, left.at[:, pl.ds(8 + nx, 8)]),
-            remote("ahpl", src_hi, right.at[:, pl.ds(0, 8)]),
-            remote("ahph", src_hi, left.at[:, pl.ds(0, 8)]),
-        ]
-
-    def layer_send(src_ref, src_index, y_at, side, slot, dst):
-        return remote(
-            side,
-            src_ref.at[pl.ds(src_index, 1), pl.ds(y_at, ny)],
-            dst.at[pl.ds(slot, 1), pl.ds(PAD, ny)],
-        )
-
-    plates_1 = plate_sends(plate_now, plate_now.at[:, lo8], plate_now.at[:, hi8], u1, u1l, u1r)
-    for number in plates_1:
-        start(number)
-    near_1 = [
-        layer_send(air_now, 0, 0, "al", nx + 2, p1),
-        layer_send(air_now, nx - 1, 0, "ah", 1, p1),
-    ]
-    far_1 = [
-        layer_send(air_now, 1, 0, "al", nx + 3, p1),
-        layer_send(air_now, nx - 2, 0, "ah", 0, p1),
-    ]
-    cols_1 = [
-        remote("pl", air_now.at[:, pl.ds(0, 8)], p1.at[pl.ds(2, nx), pl.ds(PAD + ny, 8)]),
-        remote("ph", air_now.at[:, pl.ds(ny - 8, 8)], p1.at[pl.ds(2, nx), pl.ds(0, 8)]),
-    ]
-    for number in near_1 + cols_1 + far_1:
-        start(number)
-
     for copy in loads[4:]:
         copy.wait()
     depth_start = field * nz
@@ -195,6 +153,49 @@
     clear(p1)
     clear(p2)
 
+    for copy in (loads[0], loads[2]):
+        copy.wait()
+    pl.semaphore_wait(barrier, total)
+
+    own = pl.ds(8, nx)
+
+    def plate_sends(src_own, src_lo, src_hi, mid, left, right):
+        return [
+            remote("al", src_lo, mid.at[:, pl.ds(8 + nx, 8)]),
+            remote("ah", src_hi, mid.at[:, pl.ds(0, 8)]),
+            remote("pl", src_own, right.at[:, own]),
+            remote("ph", src_own, left.at[:, own]),
+            remote("alpl", src_lo, right.at[:, pl.ds(8 + nx, 8)]),
+            remote("alph", src_lo, left.at[:, pl.ds(8 + nx, 8)]),
+            remote("ahpl", src_hi, right.at[:, pl.ds(0, 8)]),
+            remote("ahph", src_hi, left.at[:, pl.ds(0, 8)]),
+        ]
+
+    def layer_send(src_ref, src_index, y_at, side, slot, dst):
+        return remote(
+            side,
+            src_ref.at[pl.ds(src_index, 1), pl.ds(y_at, ny)],
+            dst.at[pl.ds(slot, 1), pl.ds(PAD, ny)],
+        )
+
+    plates_1 = plate_sends(u1.at[:, own], u1.at[:, pl.ds(8, 8)], u1.at[:, pl.ds(nx, 8)], u1, u1l, u1r)
+    for number in plates_1:
+        start(number)
+    near_1 = [
+        layer_send(p1, 2, PAD, "al", nx + 2, p1),
+        layer_send(p1, nx + 1, PAD, "ah", 1, p1),
+    ]
+    far_1 = [
+        layer_send(p1, 3, PAD, "al", nx + 3, p1),
+        layer_send(p1, nx, PAD, "ah", 0, p1),
+    ]
+    cols_1 = [
+        remote("pl", p1.at[pl.ds(2, nx), pl.ds(PAD, 8)], p1.at[pl.ds(2, nx), pl.ds(PAD + ny, 8)]),
+        remote("ph", p1.at[pl.ds(2, nx), pl.ds(ny, 8)], p1.at[pl.ds(2, nx), pl.ds(0, 8)]),
+    ]
+    for number in near_1 + cols_1 + far_1:
+        start(number)
+
     def prepare(value, x, sel):
         pieces = split_cat(value, 1)
         mx[x] = jnp.dot(pieces, band[...], preferred_element_type=F32)
@@ -203,18 +204,24 @@
         )
         sel[pl.ds(x * 8, 8), :] = chosen[:8]
 
-    def advance(now, back, x):
-        nearest = (now[x + 1, pl.ds(PAD, ny), :] + now[x + 3, pl.ds(PAD, ny), :]) + (
-            now[x + 2, pl.ds(PAD - 1, ny), :] + now[x + 2, pl.ds(PAD + 1, ny), :]
-        )
-        farther = (now[x, pl.ds(PAD, ny), :] + now[x + 4, pl.ds(PAD, ny), :]) + (
-            now[x + 2, pl.ds(PAD - 2, ny), :] + now[x + 2, pl.ds(PAD + 2, ny), :]
-        )
-        pushed = lax.dot_general(
+    def base(now, back, back_at, x, y0, count):
+        at = PAD + y0
+        nearest = (now[x + 1, pl.ds(at, count), :] + now[x + 3, pl.ds(at, count), :]) + (
+            now[x + 2, pl.ds(at - 1, count), :] + now[x + 2, pl.ds(at + 1, count), :]
+        )
+        farther = (now[x, pl.ds(at, count), :] + now[x + 4, pl.ds(at, count), :]) + (
+            now[x + 2, pl.ds(at - 2, count), :] + now[x + 2, pl.ds(at + 2, count), :]
+        )
+        held = back[x + back_at[0], pl.ds(y0 + back_at[1], count), :]
+        return ((16.0 * nearest - farther) + mx[x, pl.ds(y0, count), :]) * (1.0 / 60.0) - held
+
+    def pushed(x):
+        return lax.dot_general(
             split_cat(drive[pl.ds(x * 8, 8), :], 0), weights[...],
             (((0,), (0,)), ((), ())), preferred_element_type=F32,
-        )
-        return ((16.0 * nearest - farther) + (mx[x] + pushed)) * (1.0 / 60.0) - back
+        ) * (1.0 / 60.0)
+
+    mid_rows = ny - 16
 
     row_at = lax.broadcasted_iota(jnp.int32, (nx + 16, ny), 0) + (air * nx - 8)
     lane_at = lax.broadcasted_iota(jnp.int32, (nx + 16, ny), 1)
@@ -254,15 +261,15 @@
         for j in range(2):
             drive[pl.ds(plates + j, nx, stride=8), :] = sel_in[pl.ds(plates + j, nx, stride=8), :]
 
-    loads[0].wait()
-
     for x in range(nx):
         prepare(p1[x + 2, pl.ds(PAD, ny), :], x, sel_1)
-
     swap_1 = remote("f", sel_1, sel_1_in)
     start(swap_1)
-    for copy in loads[1:4]:
-        copy.wait()
+    loads[1].wait()
+    loads[3].wait()
+    first = (p1, p0, (0, 0))
+    for x in range(2, nx - 2):
+        p2[x + 2, pl.ds(PAD + 8, mid_rows), :] = base(*first, x, 8, mid_rows)
     for number in plates_1:
         arrive(number)
     arrive(swap_1)
@@ -277,39 +284,40 @@
     for number in cols_1:
         arrive(number)
 
-    def first(x):
-        value = advance(p1, p0[x], x)
-        p2[x + 2, pl.ds(PAD, ny), :] = value
-        prepare(value, x, sel_2)
+    def whole(x):
+        p2[x + 2, pl.ds(PAD, ny), :] = base(*first, x, 0, ny) + pushed(x)
 
     arrive(near_1[1])
-    first(1)
+    whole(1)
     far_low = layer_send(p2, 3, PAD, "al", nx + 3, p2)
     start(far_low)
     arrive(near_1[0])
-    first(nx - 2)
+    whole(nx - 2)
     far_high = layer_send(p2, nx, PAD, "ah", 0, p2)
     start(far_high)
-
-    for x in range(2, nx - 2):
-        first(x)
-
     arrive(far_1[1])
-    first(0)
+    whole(0)
     near_low = layer_send(p2, 2, PAD, "al", nx + 2, p2)
     start(near_low)
     arrive(far_1[0])
-    first(nx - 1)
+    whole(nx - 1)
     near_high = layer_send(p2, nx + 1, PAD, "ah", 1, p2)
     start(near_high)
-    swap_2 = remote("f", sel_2, sel_2_in)
-    start(swap_2)
+    for x in range(2, nx - 2):
+        more = pushed(x)
+        p2[x + 2, pl.ds(PAD, 8), :] = base(*first, x, 0, 8) + more[:8]
+        p2[x + 2, pl.ds(PAD + ny - 8, 8), :] = base(*first, x, ny - 8, 8) + more[ny - 8 :]
+        p2[x + 2, pl.ds(PAD + 8, mid_rows), :] += more[8 : ny - 8]
     cols_2 = [
         remote("pl", p2.at[pl.ds(2, nx), pl.ds(PAD, 8)], p2.at[pl.ds(2, nx), pl.ds(PAD + ny, 8)]),
         remote("ph", p2.at[pl.ds(2, nx), pl.ds(ny, 8)], p2.at[pl.ds(2, nx), pl.ds(0, 8)]),
     ]
     for number in cols_2:
         start(number)
+    for x in range(nx):
+        prepare(p2[x + 2, pl.ds(PAD, ny), :], x, sel_2)
+    swap_2 = remote("f", sel_2, sel_2_in)
+    start(swap_2)
     stores = [
         pltpu.make_async_copy(p2.at[pl.ds(2, nx), pl.ds(PAD, ny)], out_before, local_sem.at[0]),
         pltpu.make_async_copy(u2.at[:, own], out_plate_before, local_sem.at[1]),
@@ -317,6 +325,9 @@
     for copy in stores:
         copy.start()
 
+    second = (p2, p1, (2, PAD))
+    for x in range(2, nx - 2):
+        out_after[x, pl.ds(8, mid_rows), :] = base(*second, x, 8, mid_rows)
     for number in plates_2:
         arrive(number)
     arrive(swap_2)
@@ -325,23 +336,27 @@
             u2, u2l, u2r, lambda k, mask: mask * u1[k, own, :], sel_2, sel_2_in, k
         )
     take_edges(sel_2_in)
+    for x in range(nx):
+        more = pushed(x)
+        if 2 <= x < nx - 2:
+            out_after[x, pl.ds(0, 8), :] = more[:8]
+            out_after[x, pl.ds(ny - 8, 8), :] = more[ny - 8 :]
+            out_after[x, pl.ds(8, mid_rows), :] += more[8 : ny - 8]
+        else:
+            out_after[x] = more
     for number in cols_2:
         arrive(number)
-
-    def second(x):
-        out_after[x] = advance(p2, p1[x + 2, pl.ds(PAD, ny), :], x)
-
     for x in range(2, nx - 2):
-        second(x)
-
+        out_after[x, pl.ds(0, 8), :] += base(*second, x, 0, 8)
+        out_after[x, pl.ds(ny - 8, 8), :] += base(*second, x, ny - 8, 8)
     arrive(far_high)
     arrive(near_high)
-    second(0)
-    second(1)
+    for x in (0, 1):
+        out_after[x] += base(*second, x, 0, ny)
     arrive(far_low)
     arrive(near_low)
-    second(nx - 2)
-    second(nx - 1)
+    for x in (nx - 2, nx - 1):
+        out_after[x] += base(*second, x, 0, ny)
     for number in range(len(made)):
         sent(number)
     for copy in stores:

time: 19 us -> 15.8 us (0.83)
  Pallas kernels: 18.2 us -> 15 us
    pallas_call x1, Pallas kernels: 16.8 us -> 13.6 us  [on_device(): pl.pallas_call(functools.partial(kernel, counts), out_shape=(held_air, he...]
where the time goes in v3:
time: 15.8 us; the launch traced here: 15.6 us
  Pallas kernels  15 us (95%)
  between operations  0.64 us (4%)
    pallas_call x1, Pallas kernels, on_device(): pl.pallas_call(functools.partial(kernel, counts), out_shape=(held_air, he...  13.6 us
    pallas_call x1, Pallas kernels, on_device(): pl.pallas_call(put_kernel, out_shape=(air, air, plate, plate), in_specs=[...  1.36 us

profile of v3, /device:TPU:0, one launch (start us, length us, event | category | flops | bytes accessed | tf_op | source)
XLA Modules:
  0.0 15.6 jit_solution(188418946815545337)
XLA Ops:
  0.6 13.6 %shard_map.102 = (f32[16,128,128]{2,1,0:T(8,128)S(1)}, f32[16,128,128]{2,1,0:T(8,128)S(1)}, f32[3,16,128]{2,1,0:T(8,128)S(1)}, f32[3,16,128]{2,1,0:T(8,128)S(1)}) custom-call(f32[16,128,128]{2,1,0:T(8,128)} %air_prev.1, f32[16,128,128]{2,1,0:T(8,128)} %air_now.1, f32[3,16,128]{2,1,0:T(8,128)} %plate_prev.1, f32[3,16,128]{2,1,0:T(8,128)} %plate_now.1, ...), custom_call_target="tpu_custom_call" | custom-call | flops 13107200 | bytes 4194304 | tf_op jit(solution)/shard_map/pallas_call | solution.py:395
  14.2 1.4 %shard_map.103 = (f32[16,128,128]{2,1,0:T(8,128)}, f32[16,128,128]{2,1,0:T(8,128)}, f32[3,16,128]{2,1,0:T(8,128)}, f32[3,16,128]{2,1,0:T(8,128)}) custom-call(f32[16,128,128]{2,1,0:T(8,128)S(1)} %get-tuple-element.8.refs_0_, f32[16,128,128]{2,1,0:T(8,128)S(1)} %get-tuple-element.9.refs_1_, f32[3,16,128]{2,1,0:T(8,128)S(1)} %get-tuple-element.10.refs_2_, ...), custom_call_target="tpu_custom_call" | custom-call | bytes 4194304 | tf_op jit(solution)/shard_map/pallas_call | solution.py:420

commit v4 on v3

--- a/solution.py
+++ b/solution.py
@@ -87,15 +87,23 @@
         when(has[side], lambda: copy.wait_send())
 
     loads = [
-        pltpu.make_async_copy(air_now, p1.at[pl.ds(2, nx), pl.ds(PAD, ny)], local_sem.at[0]),
+        pltpu.make_async_copy(
+            air_now.at[pl.ds(2, nx - 4)], p1.at[pl.ds(4, nx - 4), pl.ds(PAD, ny)], local_sem.at[0]
+        ),
         pltpu.make_async_copy(air_prev, p0, local_sem.at[1]),
         pltpu.make_async_copy(plate_now, u1.at[:, pl.ds(8, nx)], local_sem.at[2]),
         pltpu.make_async_copy(plate_prev, u0, local_sem.at[3]),
         pltpu.make_async_copy(height_in, height, local_sem.at[4]),
         pltpu.make_async_copy(rows_in, rows, local_sem.at[5]),
         pltpu.make_async_copy(cols_in, cols, local_sem.at[6]),
-    ]
-    for copy in loads:
+        pltpu.make_async_copy(
+            air_now.at[pl.ds(0, 2)], p1.at[pl.ds(2, 2), pl.ds(PAD, ny)], local_sem.at[7]
+        ),
+        pltpu.make_async_copy(
+            air_now.at[pl.ds(nx - 2, 2)], p1.at[pl.ds(nx, 2), pl.ds(PAD, ny)], local_sem.at[8]
+        ),
+    ]
+    for copy in [loads[i] for i in (2, 7, 8, 4, 5, 6, 0, 1, 3)]:
         copy.start()
 
     barrier = pltpu.get_barrier_semaphore()
@@ -105,7 +113,7 @@
             pl.semaphore_signal(barrier, inc=1, device_id=target, device_id_type=MESH)
         when(has[side], hail)
         total = total + (1 if has[side] is None else has[side].astype(jnp.int32))
-    for copy in loads[4:]:
+    for copy in loads[4:7]:
         copy.wait()
     depth_start = field * nz
     lane8 = lax.broadcasted_iota(jnp.int32, (8, nz), 1)
@@ -153,7 +161,7 @@
     clear(p1)
     clear(p2)
 
-    for copy in (loads[0], loads[2]):
+    for copy in (loads[2], loads[7], loads[8]):
         copy.wait()
     pl.semaphore_wait(barrier, total)
 
@@ -193,7 +201,10 @@
         remote("pl", p1.at[pl.ds(2, nx), pl.ds(PAD, 8)], p1.at[pl.ds(2, nx), pl.ds(PAD + ny, 8)]),
         remote("ph", p1.at[pl.ds(2, nx), pl.ds(ny, 8)], p1.at[pl.ds(2, nx), pl.ds(0, 8)]),
     ]
-    for number in near_1 + cols_1 + far_1:
+    for number in near_1 + far_1:
+        start(number)
+    loads[0].wait()
+    for number in cols_1:
         start(number)
 
     def prepare(value, x, sel):
@@ -368,9 +379,17 @@
 
 def put_kernel(*refs):
     count = (len(refs) - 1) // 2
-    copies = [
-        pltpu.make_async_copy(refs[i], refs[count + i], refs[-1].at[i]) for i in range(count)
-    ]
+    copies = []
+    for i in range(count):
+        size = refs[i].shape[0]
+        parts = 4 if size % 4 == 0 else 1
+        for j in range(parts):
+            piece = pl.ds(j * (size // parts), size // parts)
+            copies.append(
+                pltpu.make_async_copy(
+                    refs[i].at[piece], refs[count + i].at[piece], refs[-1].at[len(copies)]
+                )
+            )
     for copy in copies:
         copy.start()
     for copy in copies:
@@ -406,7 +425,7 @@
             pltpu.SMEM((plates,), jnp.int32),
             pltpu.SMEM((2, plates), jnp.int32),
             pltpu.SMEM((2, plates), jnp.int32),
-            pltpu.SemaphoreType.DMA((7,)),
+            pltpu.SemaphoreType.DMA((9,)),
             pltpu.SemaphoreType.DMA((REMOTES,)),
             pltpu.SemaphoreType.DMA((REMOTES,)),
         ],
@@ -422,7 +441,7 @@
         out_shape=(air, air, plate, plate),
         in_specs=[pl.BlockSpec(memory_space=pltpu.VMEM)] * 4,
         out_specs=(stored,) * 4,
-        scratch_shapes=[pltpu.SemaphoreType.DMA((4,))],
+        scratch_shapes=[pltpu.SemaphoreType.DMA((16,))],
         cost_estimate=pl.CostEstimate(
             flops=0, bytes_accessed=16 * nx * ny * nz, transcendentals=0
         ),

time: 15.8 us -> 15.9 us (level)
  no operation moved by 1% of the time
where the time goes in v4:
time: 15.9 us; the launch traced here: 15.7 us
  Pallas kernels  15.1 us (95%)
  between operations  0.64 us (4%)
    pallas_call x1, Pallas kernels, on_device(): pl.pallas_call(functools.partial(kernel, counts), out_shape=(held_air, he...  13.6 us
    pallas_call x1, Pallas kernels, on_device(): pl.pallas_call(put_kernel, out_shape=(air, air, plate, plate), in_specs=[...  1.45 us

profile of v4, /device:TPU:0, one launch (start us, length us, event | category | flops | bytes accessed | tf_op | source)
XLA Modules:
  0.0 15.7 jit_solution(4266603535629035799)
XLA Ops:
  0.6 13.6 %shard_map.102 = (f32[16,128,128]{2,1,0:T(8,128)S(1)}, f32[16,128,128]{2,1,0:T(8,128)S(1)}, f32[3,16,128]{2,1,0:T(8,128)S(1)}, f32[3,16,128]{2,1,0:T(8,128)S(1)}) custom-call(f32[16,128,128]{2,1,0:T(8,128)} %air_prev.1, f32[16,128,128]{2,1,0:T(8,128)} %air_now.1, f32[3,16,128]{2,1,0:T(8,128)} %plate_prev.1, f32[3,16,128]{2,1,0:T(8,128)} %plate_now.1, ...), custom_call_target="tpu_custom_call" | custom-call | flops 13107200 | bytes 4194304 | tf_op jit(solution)/shard_map/pallas_call | solution.py:414
  14.3 1.5 %shard_map.103 = (f32[16,128,128]{2,1,0:T(8,128)}, f32[16,128,128]{2,1,0:T(8,128)}, f32[3,16,128]{2,1,0:T(8,128)}, f32[3,16,128]{2,1,0:T(8,128)}) custom-call(f32[16,128,128]{2,1,0:T(8,128)S(1)} %get-tuple-element.8.refs_0_, f32[16,128,128]{2,1,0:T(8,128)S(1)} %get-tuple-element.9.refs_1_, f32[3,16,128]{2,1,0:T(8,128)S(1)} %get-tuple-element.10.refs_2_, ...), custom_call_target="tpu_custom_call" | custom-call | bytes 4194304 | tf_op jit(solution)/shard_map/pallas_call | solution.py:439
